TPU v7x, 32 devices: a whole 2x2x4 slice. The times are simulated.
32 devices in a mesh: tm: 4 (over x, core), space: 8 (over z, y).
Axes of the slice: x: 2, y: 2, z: 4, core: 2. Of those that a mesh axis runs over, the one named last changes fastest.
Arguments:
- vectors: bfloat16 [4, 2, 8, 3, 256, 128], P('tm', None, 'space'), may hold values from -12 to 12
- gauge_links: float32 [4, 3, 2, 8, 3, 3, 128], P('tm', None, None, 'space'), may hold values from -2.5 to 2.5
- perambulator: bfloat16 [4, 64, 2, 256, 256], P('tm', 'space'), may hold values from -0.375 to 0.375
- directions: int32 [4], P('tm'), may hold values from 0 to 2
- momentum: int32 [3], replicated, may hold values from -2 to 2
- source_list: int32 [4], replicated, may hold values from 0 to 3, each once
Outputs:
- elementals: bfloat16 [4, 256, 2, 256], P('tm', 'space')
- correlator: float32 [2, 4, 4], P(None, 'tm')
Inputs may be any that keep to these rules, and one draw needn't show every extreme that they name: `directions`: 0, 1, 2 stand for x, y, z. `source_list`: each timeslice is the source of exactly one slot.
All inputs are finite; a program needn't handle non-finite values.
Results may differ from a plain program's by a relative error of at most 0.019.
Values may be sent and summed in bfloat16 or wider, within the bound.
A program may use at most 64 MiB of HBM per device.

v0:
```python
import math

import jax
import jax.numpy as jnp
from jax import lax
from jax.sharding import PartitionSpec as P

NV = 256
NS = 4
SX = 16
SY = 8
SMEAR = 2


smear_kappa = 0.05


def shifted(block, axis, distance):
    devices = range(lax.axis_size(axis))
    route = [((i - distance) % len(devices), i) for i in devices]
    return lax.ppermute(block, axis, route)


def colour_apply(link_field, colour_field, adjoint):
    if adjoint:
        link_real = jnp.swapaxes(link_field[0], 1, 2)
        link_imag = -jnp.swapaxes(link_field[1], 1, 2)
    else:
        link_real = link_field[0]
        link_imag = link_field[1]

    def contract(matrix, vector):
        return jnp.sum(matrix[:, :, :, None, :] * vector[:, None, :, :, :], axis=2)

    out_real = contract(link_real, colour_field[0]) - contract(link_imag, colour_field[1])
    out_imag = contract(link_real, colour_field[1]) + contract(link_imag, colour_field[0])
    return jnp.stack([out_real, out_imag])


def ahead_x(colour_field):
    column = jnp.arange(colour_field.shape[-1]) % SX
    return jnp.where(
        column == SX - 1,
        jnp.roll(colour_field, SX - 1, axis=-1),
        jnp.roll(colour_field, -1, axis=-1),
    )


def behind_x(colour_field):
    column = jnp.arange(colour_field.shape[-1]) % SX
    return jnp.where(
        column == 0, jnp.roll(colour_field, 1 - SX, axis=-1), jnp.roll(colour_field, 1, axis=-1)
    )


def upper_plane(colour_field):
    arriving = shifted(colour_field, "space", -1)
    return jnp.concatenate([colour_field[:, 1:], arriving], axis=1)


def lower_plane(colour_field):
    arriving = shifted(colour_field, "space", 1)
    return jnp.concatenate([arriving, colour_field[:, :-1]], axis=1)


def smear_once(smeared, link_set):
    colour_field = smeared.astype(jnp.float32)
    summed = -6.0 * colour_field
    for direction in range(3):
        link_field = link_set[direction]
        if direction == 0:
            incoming = ahead_x(colour_field)
        elif direction == 1:
            incoming = jnp.roll(colour_field, -SX, axis=-1)
        else:
            incoming = upper_plane(smeared).astype(jnp.float32)
        carried = colour_apply(link_field, colour_field, True)
        if direction == 0:
            outgoing = behind_x(carried)
        elif direction == 1:
            outgoing = jnp.roll(carried, SX, axis=-1)
        else:
            outgoing = lower_plane(carried.astype(jnp.bfloat16)).astype(jnp.float32)
        summed = summed + colour_apply(link_field, incoming, False) + outgoing
    return (colour_field + smear_kappa * summed).astype(jnp.bfloat16)


def covariant_step(smeared, link_set, pick):
    colour_field = smeared.astype(jnp.float32)
    link_field = lax.dynamic_index_in_dim(link_set, pick, 0, keepdims=False)
    along_z = upper_plane(smeared).astype(jnp.float32)
    incoming = jnp.where(
        pick == 0,
        ahead_x(colour_field),
        jnp.where(pick == 1, jnp.roll(colour_field, -SX, axis=-1), along_z),
    )
    carried = colour_apply(link_field, colour_field, True)
    back_z = lower_plane(carried.astype(jnp.bfloat16)).astype(jnp.float32)
    outgoing = jnp.where(
        pick == 0, behind_x(carried), jnp.where(pick == 1, jnp.roll(carried, SX, axis=-1), back_z)
    )
    return colour_apply(link_field, incoming, False) - outgoing


def phase_angle(momentum, plane_index, extent):
    site_index = jnp.arange(SX * SY)
    column = (site_index % SX).astype(jnp.float32)
    row_index = (site_index // SX).astype(jnp.float32)
    moment = momentum.astype(jnp.float32)
    return (
        2.0
        * math.pi
        * (
            moment[0] * column[None, :] / SX
            + moment[1] * row_index[None, :] / SY
            + moment[2] * plane_index.astype(jnp.float32)[:, None] / extent
        )
    )


def project_half(gradient, angle_grid):
    cosine = jnp.cos(angle_grid)[:, None, None, :]
    sine_part = jnp.sin(angle_grid)[:, None, None, :]
    return jnp.stack(
        [
            cosine * gradient[0] + sine_part * gradient[1],
            cosine * gradient[1] - sine_part * gradient[0],
        ]
    ).astype(jnp.bfloat16)


def pair_up(projected):
    return jnp.stack([projected, jnp.stack([projected[1], -projected[0]])])


def per_device(vectors, gauge_links, perambulator, directions, momentum, source_list):
    smeared = vectors[0]
    link_set = gauge_links[0]
    block_set = perambulator[0]
    planes = smeared.shape[1]
    vector_count = smeared.shape[3]
    space_count = lax.axis_size("space")
    space_index = lax.axis_index("space")
    for sweep_index in range(SMEAR):
        smeared = smear_once(smeared, link_set)
    gradient = covariant_step(smeared, link_set, directions[0])
    plane_index = space_index * planes + jnp.arange(planes)
    angle_grid = phase_angle(momentum, plane_index, planes * space_count)
    projected = project_half(gradient, angle_grid)
    paired = pair_up(projected)
    scale_factor = 1.0 / math.sqrt(3 * SX * SY * planes * space_count)
    row_total = vector_count // space_count
    partial_value = jnp.einsum(
        "rzcas,orzcbs->aob", smeared, paired, preferred_element_type=jnp.float32
    )
    summed = lax.psum(partial_value, "space")
    elemental = (summed * scale_factor).astype(jnp.bfloat16)
    own_rows = lax.dynamic_slice_in_dim(elemental, space_index * row_total, row_total, 0)
    slot_index = space_index // (space_count // lax.axis_size("tm"))
    source = source_list[slot_index]
    gathered = lax.all_gather(elemental[None], "tm", axis=0, tiled=True)
    partner = lax.dynamic_index_in_dim(gathered, source, 0, keepdims=False)
    left_side = jnp.stack(
        [
            jnp.stack([elemental[:, 0], -elemental[:, 1]], 1),
            jnp.stack([elemental[:, 1], elemental[:, 0]], 1),
        ]
    )
    first = jnp.einsum(
        "pirk,brkj->pbij", left_side, block_set, preferred_element_type=jnp.float32
    ).astype(jnp.bfloat16)
    right_side = jnp.stack(
        [jnp.stack([partner[:, 0], partner[:, 1]]), jnp.stack([-partner[:, 1], partner[:, 0]])]
    )
    second = jnp.einsum("pbik,pqkj->qbij", first, right_side, preferred_element_type=jnp.float32)
    block_real = block_set[:, 0].astype(jnp.float32)
    block_imag = block_set[:, 1].astype(jnp.float32)
    trace_real = jnp.sum(second[0] * block_real + second[1] * block_imag)
    trace_imag = jnp.sum(second[1] * block_real - second[0] * block_imag)
    pair_value = jnp.stack([trace_real, trace_imag]) / (NS * NV)
    one_hot = (jnp.arange(source_list.shape[0]) == source).astype(jnp.float32)
    spread = pair_value[:, None] * one_hot[None, :]
    correlator = lax.psum(spread, "space")
    return (own_rows[None], correlator[:, None, :])


def solution(mesh):
    in_specs = (
        P("tm", None, "space", None, None, None),
        P("tm", None, None, "space", None, None, None),
        P("tm", "space", None, None, None),
        P("tm"),
        P(),
        P(),
    )
    out_specs = (P("tm", "space", None, None), P(None, "tm", None))
    return jax.shard_map(
        per_device, mesh=mesh, in_specs=in_specs, out_specs=out_specs, check_vma=False
    )
```

profile of v0, /device:TPU:0, one launch (start us, length us, event | category | flops | bytes accessed | tf_op | source)
XLA Modules:
  0.0 220.9 jit_solution(809000771817749849)
XLA Ops:
  7.9 1.1 bitcast_convert_fusion.2
  9.0 0.7 negate_bitcast_fusion
  9.7 0.6 copy_bitcast_fusion.8
  10.3 2.0 multiply_reduce_fusion.35
  12.5 0.8 pad_maximum_fusion.7
  13.3 3.0 %collective-permute-start.1 = (bf16[2,1,3,256,128]{4,3,2,1,0:T(8,128)(2,1)}, bf16[2,1,3,256,128]{4,3,2,1,0:T(8,128)(2,1)}, u32[]{:S(2)}, u32[]{:S(2)}) collective-permute-start(bf16[2,1,3,256,128]{4,3,2,1,0:T(8,128)(2,1)} %pad_maximum_fusion.7), channel_id=1, source_target_pairs={{7,0},{0,1},{1,2},{2,3},{3,4},{4,5},{5,6},{6,7},{15,8},{8,9},{9,10... | collective-permute-start | bytes 1179656 | tf_op jit(solution)/shard_map/ppermute | solution.py:21
  16.2 3.1 %collective-permute-start = (bf16[2,1,3,256,128]{4,3,2,1,0:T(8,128)(2,1)S(1)}, bf16[2,1,3,256,128]{4,3,2,1,0:T(8,128)(2,1)}, u32[]{:S(2)}, u32[]{:S(2)}) collective-permute-start(bf16[2,1,3,256,128]{4,3,2,1,0:T(8,128)(2,1)S(1)} %bitcast.303), channel_id=1, source_target_pairs={{1,0},{2,1},{3,2},{4,3},{5,4},{6,5},{7,6},{0,7},{9,8},{10,9},{11,1... | collective-permute-start | bytes 1179656 | tf_op jit(solution)/shard_map/ppermute | solution.py:21
  19.4 1.2 slice.423
  20.9 0.9 fusion.15
  21.8 1.2 fusion.14
  23.6 0.5 copy-done.45
  24.1 0.5 maximum_select_fusion
  24.6 0.9 slice_bitcast_fusion.18
  25.5 0.7 fusion.82
  26.2 1.1 add_bitcast_fusion.7
  27.3 1.2 subtract_bitcast_fusion.7
  28.8 0.4 copy-done.39
  29.2 0.4 multiply_reduce_fusion.47
  29.8 0.8 add_bitcast_fusion.8
  30.6 0.8 subtract_bitcast_fusion.8
  31.5 1.2 multiply_reduce_fusion.55
  32.7 0.8 add_bitcast_fusion.10
  33.5 0.6 copy_bitcast_fusion
  34.6 1.9 fusion.74
  36.5 0.6 broadcast_compare_fusion
  37.1 0.6 copy.97
  38.0 1.2 subtract_bitcast_fusion.10
  39.2 1.0 convert_element_type.150
  40.3 0.4 multiply_reduce_fusion.39
  40.8 0.5 copy-done.7
  41.3 0.5 copy-done
  42.3 1.7 fusion.80
  44.0 2.0 collective-permute-start.2
  46.3 0.6 copy-done.11
  47.0 1.2 multiply_reduce_fusion.11
  49.7 0.5 maximum_select_fusion.1
  50.6 0.4 copy-done.23
  51.0 0.4 multiply_reduce_fusion.23
  51.5 0.6 copy-done.27
  52.1 0.4 multiply_reduce_fusion.31
  53.1 9.9 %collective-permute-done.2 = bf16[2,1,3,256,128]{4,3,2,1,0:T(8,128)(2,1)S(1)} collective-permute-done((bf16[2,1,3,256,128]{4,3,2,1,0:T(8,128)(2,1)S(1)}, bf16[2,1,3,256,128]{4,3,2,1,0:T(8,128)(2,1)S(1)}, u32[]{:S(2)}, u32[]{:S(2)}) %collective-permute-start.2) | collective-permute-done | bytes 393248 | tf_op jit(solution)/shard_map/ppermute | solution.py:21
  63.2 0.4 multiply_reduce_fusion.15
  63.6 0.8 fusion.78
  65.2 3.8 %collective-permute-start.4 = (bf16[2,1,3,256,128]{4,3,2,1,0:T(8,128)(2,1)S(1)}, bf16[2,1,3,256,128]{4,3,2,1,0:T(8,128)(2,1)S(1)}, u32[]{:S(2)}, u32[]{:S(2)}) collective-permute-start(bf16[2,1,3,256,128]{4,3,2,1,0:T(8,128)(2,1)S(1)} %get-tuple-element.99), channel_id=1, source_target_pairs={{1,0},{2,1},{3,2},{4,3},{5,4},{6,5},{7,6},{0,7},{9,8},{10,9},{11,1... | collective-permute-start | bytes 1179656 | tf_op jit(solution)/shard_map/ppermute | solution.py:21
  69.1 0.4 multiply_reduce_fusion.3
  70.6 6.9 %collective-permute-done.4 = bf16[2,1,3,256,128]{4,3,2,1,0:T(8,128)(2,1)S(1)} collective-permute-done((bf16[2,1,3,256,128]{4,3,2,1,0:T(8,128)(2,1)S(1)}, bf16[2,1,3,256,128]{4,3,2,1,0:T(8,128)(2,1)S(1)}, u32[]{:S(2)}, u32[]{:S(2)}) %collective-permute-start.4) | collective-permute-done | bytes 393248 | tf_op jit(solution)/shard_map/ppermute | solution.py:21
  77.5 0.7 fusion.47
  78.3 0.6 copy-done.33
  78.9 0.4 multiply_reduce_fusion.7
  79.4 4.0 %collective-permute-done.5 = bf16[2,1,3,256,128]{4,3,2,1,0:T(8,128)(2,1)S(1)} collective-permute-done((bf16[2,1,3,256,128]{4,3,2,1,0:T(8,128)(2,1)S(1)}, bf16[2,1,3,256,128]{4,3,2,1,0:T(8,128)(2,1)S(1)}, u32[]{:S(2)}, u32[]{:S(2)}) %collective-permute-start.5) | collective-permute-done | bytes 393248 | tf_op jit(solution)/shard_map/ppermute | solution.py:21
  83.4 0.7 fusion.24
  84.5 1.2 convolution_bitcast_fusion.1
  85.8 75.7 %all-reduce.2.cloned.1.call-done = f32[256,2,256]{2,0,1:T(8,128)} async-done(((f32[256,2,256]{2,0,1:T(8,128)}), f32[256,2,256]{2,0,1:T(8,128)}) %all-reduce.2.cloned.1.call-update) | async-done | bytes 524304 | tf_op jit(solution)/shard_map/psum | solution.py:156
  161.5 1.8 multiply_convert_fusion
  163.4 0.6 dynamic_slice.16
  165.3 2.9 %copy.54 = bf16[1,8,2,256,256]{3,4,1,2,0:T(8,128)(2,1)S(1)} copy(bf16[1,8,2,256,256]{4,3,2,1,0:T(8,128)(2,1)} %param.8) | data formatting | bytes 4194304 | tf_op args[2]
  168.8 0.7 compare_convert_fusion
  169.6 9.9 %all-gather.3.cloned.1.call-done = bf16[1024,2,256]{2,0,1:T(8,128)(2,1)} async-done(((bf16[256,2,256]{2,0,1:T(8,128)(2,1)}), bf16[1024,2,256]{2,0,1:T(8,128)(2,1)}) %all-gather.3.cloned.1.call-update) | async-done | bytes 1048592 | tf_op jit(solution)/shard_map/all_gather | solution.py:161
  179.5 1.0 constant_dynamic-slice_fusion.1
  180.7 5.9 %convolution_bitcast_fusion = f32[2,8,256,256]{2,3,1,0:T(8,128)} fusion(bf16[1,8,2,256,256]{4,3,2,1,0:T(8,128)(2,1)} %param.8, bf16[1,2,256,256]{2,3,0,1:T(8,128)(2,1)S(1)} %get-tuple-element.134, bf16[1,2,256,256]{2,3,0,1:T(8,128)(2,1)S(1)} %get-tuple-element.133, bf16[1,256,2,256]{3,1,2,0:T(8,128)(2,1)S(1)} %get-tuple-element.132, ...), kind=kOutput, calls=%fused_computation.5 | convolution fusion | flops 2150629376 | bytes 7340032 | tf_op jit(solution)/shard_map/pbik,pqkj->qbij/dot_general | solution.py:175
  186.6 3.5 %fusion.1 = (f32[]{:T(128)}, f32[]{:T(128)}) fusion(f32[2,8,256,256]{2,3,1,0:T(8,128)} %convolution_bitcast_fusion, bf16[8,2,256,256]{2,3,0,1:T(8,128)(2,1)S(1)} %bitcast.300), kind=kLoop, calls=%fused_computation.7 | loop fusion | flops 5242878 | bytes 6291464 | tf_op jit(solution)/shard_map/reduce_sum | solution.py:178
  190.1 1.4 maximum_multiply_fusion
  191.5 0.6 copy.56
  192.2 21.9 %psum.15 = f32[2,1,4]{2,0,1:T(2,128)} all-reduce(f32[2,1,4]{2,0,1:T(2,128)S(1)} %multiply_bitcast_fusion), channel_id=1, replica_groups=mesh['tm'=4,'space'=8] {'space'}, use_global_device_ids=true, to_apply=%region_59.60 | all-reduce | flops 8 | bytes 64 | tf_op jit(solution)/shard_map/psum | solution.py:183
  (181 shorter events, 8.5 us)
Async XLA Ops:
  7.2 154.4 %all-reduce.2.cloned.1.call-start = ((), (), s32[]{:S(2)}) async-start(), calls=%async_computation | async-start | bytes 1048576 | tf_op jit(solution)/shard_map/psum | solution.py:156
  7.9 1.1 copy-start.30
  9.7 2.7 %copy-start.10 = (f32[1,3,3,128]{3,2,1,0:T(4,128)}, f32[1,3,3,128]{3,2,1,0:T(4,128)S(1)}, u32[]{:S(2)}) copy-start(f32[1,3,3,128]{3,2,1,0:T(4,128)S(1)} %copy.98) | copy-start | bytes 13828
  9.7 2.6 %copy-start.12 = (f32[3,3,128]{2,1,0:T(4,128)}, f32[3,3,128]{2,1,0:T(4,128)S(1)}, u32[]{:S(2)}) copy-start(f32[3,3,128]{2,1,0:T(4,128)S(1)} %get-tuple-element.163) | copy-start | bytes 13828
  9.7 2.6 %copy-start.14 = (f32[3,3,128]{2,1,0:T(4,128)}, f32[3,3,128]{2,1,0:T(4,128)S(1)}, u32[]{:S(2)}) copy-start(f32[3,3,128]{2,1,0:T(4,128)S(1)} %get-tuple-element.164) | copy-start | bytes 13828
  9.7 2.6 %copy-start.16 = (f32[3,3,128]{2,1,0:T(4,128)}, f32[3,3,128]{2,1,0:T(4,128)S(1)}, u32[]{:S(2)}) copy-start(f32[3,3,128]{2,1,0:T(4,128)S(1)} %get-tuple-element.165) | copy-start | bytes 13828
  9.7 2.6 %copy-start.18 = (f32[3,3,128]{2,1,0:T(4,128)}, f32[3,3,128]{2,1,0:T(4,128)S(1)}, u32[]{:S(2)}) copy-start(f32[3,3,128]{2,1,0:T(4,128)S(1)} %get-tuple-element.166) | copy-start | bytes 13828
  10.3 2.0 copy-start.20
  12.3 3.9 %copy-start.4 = (bf16[1,2,1,3,256,128]{5,4,3,2,1,0:T(8,128)(2,1)S(1)}, bf16[1,2,1,3,256,128]{5,4,3,2,1,0:T(8,128)(2,1)}, u32[]{:S(2)}) copy-start(bf16[1,2,1,3,256,128]{5,4,3,2,1,0:T(8,128)(2,1)} %param.6) | copy-start | bytes 1179652
  13.3 27.5 %collective-permute-start.1 = (bf16[2,1,3,256,128]{4,3,2,1,0:T(8,128)(2,1)}, bf16[2,1,3,256,128]{4,3,2,1,0:T(8,128)(2,1)}, u32[]{:S(2)}, u32[]{:S(2)}) collective-permute-start(bf16[2,1,3,256,128]{4,3,2,1,0:T(8,128)(2,1)} %pad_maximum_fusion.7), channel_id=1, source_target_pairs={{7,0},{0,1},{1,2},{2,3},{3,4},{4,5},{5,6},{6,7},{15,8},{8,9},{9,10... | collective-permute-start | bytes 1179656 | tf_op jit(solution)/shard_map/ppermute | solution.py:21
  16.2 22.9 %collective-permute-start = (bf16[2,1,3,256,128]{4,3,2,1,0:T(8,128)(2,1)S(1)}, bf16[2,1,3,256,128]{4,3,2,1,0:T(8,128)(2,1)}, u32[]{:S(2)}, u32[]{:S(2)}) collective-permute-start(bf16[2,1,3,256,128]{4,3,2,1,0:T(8,128)(2,1)S(1)} %bitcast.303), channel_id=1, source_target_pairs={{1,0},{2,1},{3,2},{4,3},{5,4},{6,5},{7,6},{0,7},{9,8},{10,9},{11,1... | collective-permute-start | bytes 1179656 | tf_op jit(solution)/shard_map/ppermute | solution.py:21
  23.5 0.5 copy-start.45
  24.5 1.0 copy-start.48
  24.6 1.6 copy-start.41
  24.6 1.6 copy-start.42
  26.2 2.3 %copy-start.2 = (f32[2,1,3,256,112]{4,3,2,1,0:T(8,128)S(1)}, f32[2,1,3,256,112]{4,3,2,1,0:T(8,128)}, u32[]{:S(2)}) copy-start(f32[2,1,3,256,112]{4,3,2,1,0:T(8,128)} %slice.423) | copy-start | bytes 2064388
  28.5 0.7 copy-start.39
  28.5 0.7 copy-start.40
  29.2 0.6 copy-start.22
  29.2 0.6 copy-start.24
  29.8 1.6 copy-start.37
  29.8 1.6 copy-start.38
  29.8 1.6 copy-start.8
  29.8 1.6 copy-start.9
  31.4 1.2 copy-start.26
  31.4 1.2 copy-start.28
  32.7 0.8 copy-start.31
  32.7 0.8 copy-start.36
  40.3 1.0 copy-start.7
  40.7 1.2 copy-start
  40.7 1.4 copy-start.1
  40.7 1.5 copy-start.5
  40.7 1.6 copy-start.6
  40.7 1.6 copy-start.47
  44.0 19.1 %collective-permute-start.2 = (bf16[2,1,3,256,128]{4,3,2,1,0:T(8,128)(2,1)S(1)}, bf16[2,1,3,256,128]{4,3,2,1,0:T(8,128)(2,1)S(1)}, u32[]{:S(2)}, u32[]{:S(2)}) collective-permute-start(bf16[2,1,3,256,128]{4,3,2,1,0:T(8,128)(2,1)S(1)} %get-tuple-element.101), channel_id=1, source_target_pairs={{1,0},{2,1},{3,2},{4,3},{5,4},{6,5},{7,6},{0,7},{9,8},{10,9},{11,1... | collective-permute-start | bytes 1179656 | tf_op jit(solution)/shard_map/ppermute | solution.py:21
  46.2 0.7 copy-start.11
  46.2 0.7 copy-start.13
  46.2 0.7 copy-start.15
  46.3 0.7 copy-start.17
  46.3 0.7 copy-start.19
  46.3 0.7 copy-start.21
  49.1 0.6 copy-start.46
  49.2 14.4 %collective-permute-start.3 = (bf16[2,1,3,256,128]{4,3,2,1,0:T(8,128)(2,1)S(1)}, bf16[2,1,3,256,128]{4,3,2,1,0:T(8,128)(2,1)S(1)}, u32[]{:S(2)}, u32[]{:S(2)}) collective-permute-start(bf16[2,1,3,256,128]{4,3,2,1,0:T(8,128)(2,1)S(1)} %pad_maximum_fusion.8), channel_id=1, source_target_pairs={{7,0},{0,1},{1,2},{2,3},{3,4},{4,5},{5,6},{6,7},{15,8},{8,9},{9,10... | collective-permute-start | bytes 1179656 | tf_op jit(solution)/shard_map/ppermute | solution.py:21
  50.3 0.7 copy-start.23
  50.3 0.7 copy-start.25
  51.4 0.7 copy-start.27
  51.4 0.7 copy-start.29
  65.2 3.9 %copy-start.32 = (f32[3,3,128]{2,1,0:T(4,128)S(1)}, f32[3,3,128]{2,1,0:T(4,128)}, u32[]{:S(2)}) copy-start(f32[3,3,128]{2,1,0:T(4,128)} %get-tuple-element.161) | copy-start | bytes 13828
  65.2 3.9 %copy-start.35 = (f32[1,3,3,128]{3,2,1,0:T(4,128)S(1)}, f32[1,3,3,128]{3,2,1,0:T(4,128)}, u32[]{:S(2)}) copy-start(f32[1,3,3,128]{3,2,1,0:T(4,128)} %copy.97) | copy-start | bytes 13828
  65.2 12.4 %collective-permute-start.4 = (bf16[2,1,3,256,128]{4,3,2,1,0:T(8,128)(2,1)S(1)}, bf16[2,1,3,256,128]{4,3,2,1,0:T(8,128)(2,1)S(1)}, u32[]{:S(2)}, u32[]{:S(2)}) collective-permute-start(bf16[2,1,3,256,128]{4,3,2,1,0:T(8,128)(2,1)S(1)} %get-tuple-element.99), channel_id=1, source_target_pairs={{1,0},{2,1},{3,2},{4,3},{5,4},{6,5},{7,6},{0,7},{9,8},{10,9},{11,1... | collective-permute-start | bytes 1179656 | tf_op jit(solution)/shard_map/ppermute | solution.py:21
  69.9 13.5 %collective-permute-start.5 = (bf16[2,1,3,256,128]{4,3,2,1,0:T(8,128)(2,1)S(1)}, bf16[2,1,3,256,128]{4,3,2,1,0:T(8,128)(2,1)S(1)}, u32[]{:S(2)}, u32[]{:S(2)}) collective-permute-start(bf16[2,1,3,256,128]{4,3,2,1,0:T(8,128)(2,1)S(1)} %pad_maximum_fusion.9), channel_id=1, source_target_pairs={{7,0},{0,1},{1,2},{2,3},{3,4},{4,5},{5,6},{6,7},{15,8},{8,9},{9,10... | collective-permute-start | bytes 1179656 | tf_op jit(solution)/shard_map/ppermute | solution.py:21
  78.2 0.7 copy-start.33
  78.2 0.7 copy-start.34
  79.4 4.7 %copy-start.43 = (f32[128]{0:T(128)S(1)}, f32[128]{0:T(128)}, u32[]{:S(2)}) copy-start(f32[128]{0:T(128)} %get-tuple-element.151) | copy-start | bytes 1540
  79.4 4.7 %copy-start.44 = (f32[128]{0:T(128)S(1)}, f32[128]{0:T(128)}, u32[]{:S(2)}) copy-start(f32[128]{0:T(128)} %get-tuple-element.152) | copy-start | bytes 1540
  85.7 77.7 %copy-start.49 = (s32[4]{0:T(128)S(1)}, s32[4]{0:T(128)}, u32[]{:S(2)}) copy-start(s32[4]{0:T(128)} %param.11) | copy-start | bytes 52
  85.7 93.8 %all-gather.3.cloned.1.call-start = ((), (), s32[]{:S(2)}) async-start(), calls=%async_computation.1 | async-start | bytes 1310720 | tf_op jit(solution)/shard_map/all_gather | solution.py:161
  165.3 4.2 %copy-start.3 = (bf16[256,2,256]{2,0,1:T(8,128)(2,1)S(1)}, bf16[256,2,256]{2,0,1:T(8,128)(2,1)}, u32[]{:S(2)}) copy-start(bf16[256,2,256]{2,0,1:T(8,128)(2,1)} %multiply_convert_fusion) | copy-start | bytes 786436
Sparse Core Ops, SparseCore 0:
  85.8 75.6 all-reduce.1
  163.5 15.9 all-gather.2
where the time goes:
time: 222 us; the launch traced here: 221 us
  waiting for transfers between devices  107 us (48%)
  other arithmetic  37.5 us (17%)
  blocking collectives  21.9 us (10%)
  between operations  18.3 us (8%)
  local copies, waits for them, and re-layouts  17.3 us (8%)
  starting transfers between devices  12.3 us (6%)
  matrix products  7.09 us (3%)
    psum x1, waiting for transfers between devices, per_device(): summed = lax.psum(partial_value, 'space')  75.7 us
    psum x1, blocking collectives, per_device(): correlator = lax.psum(spread, 'space')  21.9 us
    ppermute x6, waiting for transfers between devices, shifted(): return lax.ppermute(block, axis, route)  20.9 us
    ppermute x6, starting transfers between devices, shifted(): return lax.ppermute(block, axis, route)  12.3 us
    all_gather x1, waiting for transfers between devices, per_device(): gathered = lax.all_gather(elemental[None], 'tm', axis=0, tiled=True)  9.91 us
    unnamed x106, local copies, waits for them, and re-layouts  9.31 us
    another operation x28, other arithmetic, colour_apply(): return jnp.stack([out_real, out_imag])  9.22 us
    reduce_sum x10, other arithmetic, contract(): return jnp.sum(matrix[:, :, :, None, :] * vector[:, None, :, :, :], axis=2)  6.87 us
  transfers between devices with their start and end apart: 8, of which 5 were waited for; matrix products, arithmetic and copies ran while one was open for 14% of the time, Pallas kernels for 0%

commit v1 on v0

v1 whole, which is shorter than its diff:
```python
import math

import jax
import jax.numpy as jnp
from jax import lax
from jax.experimental import pallas as pl
from jax.experimental.pallas import tpu as pltpu
from jax.sharding import PartitionSpec as P

NS = 4
SX = 16
SY = 8
SMEAR = 2

MESH = pl.DeviceIdType.MESH
smear_kappa = 0.05


def row_chunk(rows):
    return 16 if rows % 16 == 0 else rows


def flat_rows(block):
    count, rows, lanes = block.shape
    if rows % 16 == 0:
        return block.reshape(count * rows, lanes)
    wide = block.astype(jnp.float32).reshape(count * rows, lanes)
    return wide.astype(jnp.bfloat16)


def apply_link(link, field):
    real = []
    imag = []
    for i in range(3):
        total_real = None
        total_imag = None
        for j in range(3):
            link_real, link_imag = link(0, i, j), link(1, i, j)
            term_real = link_real * field[j] - link_imag * field[3 + j]
            term_imag = link_real * field[3 + j] + link_imag * field[j]
            total_real = term_real if j == 0 else total_real + term_real
            total_imag = term_imag if j == 0 else total_imag + term_imag
        real.append(total_real)
        imag.append(total_imag)
    return real + imag


def apply_adjoint(link, field):
    def flipped(part, i, j):
        value = link(part, j, i)
        return value if part == 0 else -value

    real = []
    imag = []
    for i in range(3):
        total_real = None
        total_imag = None
        for j in range(3):
            link_real, link_imag = link(0, j, i), link(1, j, i)
            term_real = link_real * field[j] + link_imag * field[3 + j]
            term_imag = link_real * field[3 + j] - link_imag * field[j]
            total_real = term_real if j == 0 else total_real + term_real
            total_imag = term_imag if j == 0 else total_imag + term_imag
        real.append(total_real)
        imag.append(total_imag)
    return real + imag


def ahead_x(part, column):
    return jnp.where(column == SX - 1, pltpu.roll(part, SX - 1, 1), pltpu.roll(part, SX * SY - 1, 1))


def behind_x(part, column):
    return jnp.where(column == 0, pltpu.roll(part, SX * SY - SX + 1, 1), pltpu.roll(part, 1, 1))


def ahead_y(part):
    return pltpu.roll(part, SX * SY - SX, 1)


def behind_y(part):
    return pltpu.roll(part, SX, 1)


def kernel(
    n,
    nt,
    source_ref,
    field_ref,
    gauge_ref,
    table_ref,
    block_ref,
    own_ref,
    trace_ref,
    gauge_own,
    gauge_send,
    gauge_in,
    gauge_all,
    field_in,
    once,
    twice,
    gradient,
    twice_in,
    gradient_in,
    part_send,
    part_in,
    own_send,
    rows_tm,
    rows_sink,
    source_send,
    rows_source,
    blocks,
    weight,
    trace_send,
    trace_in,
    send_sem,
    recv_sem,
    tm_send_sem,
    tm_recv_sem,
    block_sem,
):
    me = lax.axis_index("space")
    tm_me = lax.axis_index("tm")
    rows = field_ref.shape[2]
    chunk = row_chunk(rows)
    per_plane = rows // chunk
    lanes = SX * SY
    nv = n * rows

    load_blocks = pltpu.make_async_copy(block_ref, blocks, block_sem)
    load_blocks.start()

    barrier = pltpu.get_barrier_semaphore()

    def greet_space(d, carry):
        pl.semaphore_signal(
            barrier, inc=1, device_id={"space": lax.rem(me + d, n)}, device_id_type=MESH
        )
        return carry

    def greet_tm(d, carry):
        pl.semaphore_signal(
            barrier, inc=1, device_id={"tm": lax.rem(tm_me + d, nt)}, device_id_type=MESH
        )
        return carry

    lax.fori_loop(1, n, greet_space, 0)
    lax.fori_loop(1, nt, greet_tm, 0)

    for k in range(gauge_ref.shape[0]):
        gauge_own[pl.ds(3 * k, 3), :] = gauge_ref[k]
    gauge_send[...] = gauge_own[...].astype(jnp.bfloat16)
    gauge_in[me] = gauge_send[...]
    field_in[me] = field_ref[:, me]
    pl.semaphore_wait(barrier, n - 1 + nt - 1)

    def remote(kind, source, target, peer, slot):
        return pltpu.make_async_remote_copy(
            src_ref=source,
            dst_ref=target,
            send_sem=send_sem.at[kind, peer],
            recv_sem=recv_sem.at[kind, slot],
            device_id={"space": peer},
            device_id_type=MESH,
        )

    def each_peer(act):
        def step(d, carry):
            act(lax.rem(me + d, n))
            return carry

        lax.fori_loop(1, n, step, 0)

    def gauge_copy(peer, slot):
        return remote(0, gauge_send, gauge_in.at[slot], peer, slot)

    def field_copy(peer, slot):
        return remote(1, field_ref.at[:, peer], field_in.at[slot], peer, slot)

    def twice_copy(peer, slot):
        return remote(2, twice.at[peer], twice_in.at[slot], peer, slot)

    def gradient_copy(peer, slot):
        return remote(3, gradient.at[peer], gradient_in.at[slot], peer, slot)

    def part_copy(peer, slot):
        return remote(4, part_send.at[peer], part_in.at[slot], peer, slot)

    def sink_copy(peer, slot):
        return remote(5, own_send, rows_sink.at[slot], peer, slot)

    def source_copy(peer, slot):
        return remote(6, source_send.at[peer], rows_source.at[slot], peer, slot)

    def trace_copy(peer, slot):
        return remote(7, trace_send, trace_in.at[slot], peer, slot)

    def start_all(copy):
        each_peer(lambda peer: copy(peer, me).start())

    def arrive_all(copy):
        each_peer(lambda peer: copy(peer, peer).wait_recv())

    start_all(gauge_copy)
    start_all(field_copy)
    arrive_all(gauge_copy)

    def widen(z, carry):
        gauge_all[z] = gauge_in[z].astype(jnp.float32)
        return carry

    lax.fori_loop(0, n, widen, 0)
    arrive_all(field_copy)

    column = lax.broadcasted_iota(jnp.int32, (chunk, lanes), 1) % SX

    def link_at(z, direction):
        def link(part, i, j):
            return gauge_all[z, pl.ds(((direction * 2 + part) * 3 + i) * 3 + j, 1), :]

        return link

    def sweep(held, out, z, piece):
        span = pl.ds(pl.multiple_of(piece * chunk, chunk), chunk)
        above = lax.rem(z + 1, n)
        below = lax.rem(z + n - 1, n)

        def field_at(plane):
            return [held[plane, k, span, :].astype(jnp.float32) for k in range(6)]

        here = field_at(z)
        total = [-6.0 * part for part in here]

        def add(terms):
            for k in range(6):
                total[k] = total[k] + terms[k]

        add(apply_link(link_at(z, 0), [ahead_x(part, column) for part in here]))
        add([behind_x(part, column) for part in apply_adjoint(link_at(z, 0), here)])
        add(apply_link(link_at(z, 1), [ahead_y(part) for part in here]))
        add([behind_y(part) for part in apply_adjoint(link_at(z, 1), here)])
        add(apply_link(link_at(z, 2), field_at(above)))
        add(apply_adjoint(link_at(below, 2), field_at(below)))
        for k in range(6):
            out[z, k, span, :] = (here[k] + smear_kappa * total[k]).astype(jnp.bfloat16)

    def derive(z, piece):
        span = pl.ds(pl.multiple_of(piece * chunk, chunk), chunk)
        above = lax.rem(z + 1, n)
        below = lax.rem(z + n - 1, n)

        def field_at(plane):
            return [twice[plane, k, span, :].astype(jnp.float32) for k in range(6)]

        pick = table_ref[z, pl.ds(2, 1), :]
        along_x = pick == 0.0
        along_y = pick == 1.0
        along_z = pick == 2.0
        wide_x = jnp.broadcast_to(pick, (chunk, lanes)) == 0.0
        wide_y = jnp.broadcast_to(pick, (chunk, lanes)) == 1.0
        wide_z = jnp.broadcast_to(pick, (chunk, lanes)) == 2.0
        links = [link_at(z, direction) for direction in range(3)]
        link_below = link_at(below, 2)

        def chosen(part, i, j):
            return jnp.where(
                along_x,
                links[0](part, i, j),
                jnp.where(along_y, links[1](part, i, j), links[2](part, i, j)),
            )

        def chosen_back(part, i, j):
            return jnp.where(
                along_x,
                links[0](part, i, j),
                jnp.where(along_y, links[1](part, i, j), link_below(part, i, j)),
            )

        here = field_at(z)
        up = field_at(above)
        down = field_at(below)
        incoming = [
            jnp.where(
                wide_x, ahead_x(here[k], column), jnp.where(wide_y, ahead_y(here[k]), up[k])
            )
            for k in range(6)
        ]
        base = [jnp.where(wide_z, down[k], here[k]) for k in range(6)]
        forward = apply_link(chosen, incoming)
        back = apply_adjoint(chosen_back, base)
        back = [
            jnp.where(wide_x, behind_x(part, column), jnp.where(wide_y, behind_y(part), part))
            for part in back
        ]
        slope = [forward[k] - back[k] for k in range(6)]
        cosine = table_ref[z, pl.ds(0, 1), :]
        sine = table_ref[z, pl.ds(1, 1), :]
        for c in range(3):
            real, imag = slope[c], slope[3 + c]
            gradient[z, c, span, :] = (cosine * real + sine * imag).astype(jnp.bfloat16)
            gradient[z, 3 + c, span, :] = (cosine * imag - sine * real).astype(jnp.bfloat16)

    def each_piece(act):
        def step(piece, carry):
            act(piece)
            return carry

        lax.fori_loop(0, per_plane, step, 0)

    bufs = [field_in, once, twice]
    for sweep_index in range(SMEAR - 1):

        def sweep_plane(z, carry):
            each_piece(lambda piece: sweep(bufs[0], bufs[1], z, piece))
            return carry

        lax.fori_loop(0, n, sweep_plane, 0)

    def last_plane(d, carry):
        z = lax.rem(me + d, n)
        each_piece(lambda piece: sweep(once, twice, z, piece))

        @pl.when(d < n)
        def _():
            twice_copy(z, me).start()

        return carry

    lax.fori_loop(1, n + 1, last_plane, 0)
    twice_in[me] = twice[me]

    def derive_plane(d, carry):
        z = lax.rem(me + d, n)
        each_piece(lambda piece: derive(z, piece))

        @pl.when(d < n)
        def _():
            gradient_copy(z, me).start()

        return carry

    lax.fori_loop(1, n + 1, derive_plane, 0)
    gradient_in[me] = gradient[me]

    arrive_all(twice_copy)
    arrive_all(gradient_copy)
    left = jnp.concatenate([flat_rows(twice_in[:, k]) for k in range(6)], axis=1)
    parts = [flat_rows(gradient_in[:, k]) for k in range(6)]
    right_real = jnp.concatenate(parts, axis=1)
    right_imag = jnp.concatenate(parts[3:] + [-part for part in parts[:3]], axis=1)
    nt_dims = (((1,), (1,)), ((), ()))
    sum_real = lax.dot_general(left, right_real, nt_dims, preferred_element_type=jnp.float32)
    sum_imag = lax.dot_general(left, right_imag, nt_dims, preferred_element_type=jnp.float32)
    part_send[:, :, :nv] = sum_real.reshape(n, rows, nv).astype(jnp.bfloat16)
    part_send[:, :, nv:] = sum_imag.reshape(n, rows, nv).astype(jnp.bfloat16)
    part_in[me] = part_send[me]
    start_all(part_copy)
    arrive_all(part_copy)
    scale = 1.0 / math.sqrt(3 * SX * SY * n)
    summed = jnp.sum(part_in[...].astype(jnp.float32), axis=0)
    own = (summed * scale).astype(jnp.bfloat16)
    own_send[...] = own
    own_ref[...] = own
    rows_sink[me] = own
    rows_tm[tm_me] = own

    def tm_copy(peer, slot):
        return pltpu.make_async_remote_copy(
            src_ref=own_send,
            dst_ref=rows_tm.at[slot],
            send_sem=tm_send_sem.at[peer],
            recv_sem=tm_recv_sem.at[slot],
            device_id={"tm": peer},
            device_id_type=MESH,
        )

    def each_tm(act):
        def step(d, carry):
            act(lax.rem(tm_me + d, nt))
            return carry

        lax.fori_loop(1, nt, step, 0)

    each_tm(lambda peer: tm_copy(peer, tm_me).start())
    start_all(sink_copy)
    each_tm(lambda peer: tm_copy(peer, peer).wait_recv())

    def fill_source(i, carry):
        source_send[i] = rows_tm[source_ref[i // (n // nt)]]
        return carry

    lax.fori_loop(0, n, fill_source, 0)
    rows_source[me] = source_send[me]
    start_all(source_copy)
    arrive_all(sink_copy)
    load_blocks.wait()

    sink = flat_rows(rows_sink[...])
    weight[...] = jnp.zeros_like(weight)

    def one_block(q, carry):
        real = blocks[q, 0]
        imag = blocks[q, 1]
        tall = jnp.concatenate([real, -imag], axis=0)
        tall_imag = jnp.concatenate([imag, real], axis=0)
        first_real = jnp.dot(sink, tall, preferred_element_type=jnp.float32)
        first_imag = jnp.dot(sink, tall_imag, preferred_element_type=jnp.float32)
        stacked = jnp.concatenate([first_real, first_imag], axis=0).astype(jnp.bfloat16)
        tn_dims = (((0,), (0,)), ((), ()))
        weight[:, :nv] += lax.dot_general(
            stacked,
            jnp.concatenate([real, imag], axis=0),
            tn_dims,
            preferred_element_type=jnp.float32,
        )
        weight[:, nv:] += lax.dot_general(
            stacked,
            jnp.concatenate([-imag, real], axis=0),
            tn_dims,
            preferred_element_type=jnp.float32,
        )
        return carry

    lax.fori_loop(0, blocks.shape[0], one_block, 0)
    arrive_all(source_copy)
    partner = flat_rows(rows_source[...]).astype(jnp.float32)
    partner_real, partner_imag = partner[:, :nv], partner[:, nv:]
    weight_real, weight_imag = weight[:, :nv], weight[:, nv:]
    trace_real = jnp.sum(partner_real * weight_real - partner_imag * weight_imag)
    trace_imag = jnp.sum(partner_real * weight_imag + partner_imag * weight_real)
    row = lax.broadcasted_iota(jnp.int32, trace_send.shape, 0)
    lane = lax.broadcasted_iota(jnp.int32, trace_send.shape, 1)
    mine = source_ref[me // (n // nt)]
    value = jnp.where(row == 0, trace_real, jnp.where(row == 1, trace_imag, 0.0))
    value = jnp.where(lane == mine, value, 0.0) * (1.0 / (NS * nv))
    trace_send[...] = value
    trace_in[me] = value
    start_all(trace_copy)
    arrive_all(trace_copy)
    trace_ref[...] = jnp.sum(trace_in[...], axis=0)

    for copy in (
        gauge_copy,
        field_copy,
        twice_copy,
        gradient_copy,
        part_copy,
        sink_copy,
        source_copy,
        trace_copy,
    ):
        each_peer(lambda peer: copy(peer, me).wait_send())
    each_tm(lambda peer: tm_copy(peer, tm_me).wait_send())


def per_device(n, nt, vectors, gauge_links, perambulator, directions, momentum, source_list):
    nv = vectors.shape[4]
    lanes = vectors.shape[5]
    rows = nv // n
    field = vectors.reshape(6, n, rows, lanes)
    gauge = gauge_links.reshape(18, 3, lanes)
    block_set = perambulator[0]

    site = jnp.arange(lanes)
    moment = momentum.astype(jnp.float32)
    plane = jnp.arange(n).astype(jnp.float32)
    angle = (
        2.0
        * math.pi
        * (
            moment[0] * (site % SX).astype(jnp.float32)[None, :] / SX
            + moment[1] * (site // SX).astype(jnp.float32)[None, :] / SY
            + moment[2] * plane[:, None] / n
        )
    )
    pick = jnp.broadcast_to(directions[0].astype(jnp.float32), angle.shape)
    table = jnp.stack([jnp.cos(angle), jnp.sin(angle), pick, pick], axis=1)

    bf16, f32 = jnp.bfloat16, jnp.float32
    vmem = pl.BlockSpec(memory_space=pltpu.VMEM)
    smem = pl.BlockSpec(memory_space=pltpu.SMEM)
    anywhere = pl.BlockSpec(memory_space=pl.ANY)
    split = (n, 6, rows, lanes)
    count = block_set.shape[0]
    own, trace = pl.pallas_call(
        lambda *refs: kernel(n, nt, *refs),
        out_shape=(
            jax.ShapeDtypeStruct((rows, 2 * nv), bf16),
            jax.ShapeDtypeStruct((8, 128), f32),
        ),
        in_specs=[smem, vmem, vmem, vmem, anywhere],
        out_specs=(vmem, vmem),
        scratch_shapes=[
            pltpu.VMEM((64, lanes), f32),
            pltpu.VMEM((64, lanes), bf16),
            pltpu.VMEM((n, 64, lanes), bf16),
            pltpu.VMEM((n, 64, lanes), f32),
            pltpu.VMEM(split, bf16),
            pltpu.VMEM(split, bf16),
            pltpu.VMEM(split, bf16),
            pltpu.VMEM(split, bf16),
            pltpu.VMEM(split, bf16),
            pltpu.VMEM(split, bf16),
            pltpu.VMEM((n, rows, 2 * nv), bf16),
            pltpu.VMEM((n, rows, 2 * nv), bf16),
            pltpu.VMEM((rows, 2 * nv), bf16),
            pltpu.VMEM((nt, rows, 2 * nv), bf16),
            pltpu.VMEM((n, rows, 2 * nv), bf16),
            pltpu.VMEM((n, rows, 2 * nv), bf16),
            pltpu.VMEM((n, rows, 2 * nv), bf16),
            pltpu.VMEM((count, 2, nv, nv), bf16),
            pltpu.VMEM((nv, 2 * nv), f32),
            pltpu.VMEM((8, 128), f32),
            pltpu.VMEM((n, 8, 128), f32),
            pltpu.SemaphoreType.DMA((8, n)),
            pltpu.SemaphoreType.DMA((8, n)),
            pltpu.SemaphoreType.DMA((nt,)),
            pltpu.SemaphoreType.DMA((nt,)),
            pltpu.SemaphoreType.DMA,
        ],
        compiler_params=pltpu.CompilerParams(
            collective_id=0, has_side_effects=True, vmem_limit_bytes=40 * 1024 * 1024
        ),
        name="meson",
    )(source_list, field, gauge, table, block_set)
    return (own.reshape(1, rows, 2, nv), trace[:2, None, :nt])


def solution(mesh):
    in_specs = (
        P("tm", None, "space", None, None, None),
        P("tm", None, None, "space", None, None, None),
        P("tm", "space", None, None, None),
        P("tm"),
        P(),
        P(),
    )
    out_specs = (P("tm", "space", None, None), P(None, "tm", None))
    n, nt = mesh.shape["space"], mesh.shape["tm"]

    def body(*args):
        return per_device(n, nt, *args)

    return jax.shard_map(
        body, mesh=mesh, in_specs=in_specs, out_specs=out_specs, check_vma=False
    )
```

time: 222 us -> 79 us (0.36)
  waiting for transfers between devices: 107 us -> 0 us
  Pallas kernels: 0 us -> 67.5 us
  other arithmetic: 37.5 us -> 2.77 us
  blocking collectives: 21.9 us -> 0 us
  between operations: 18.3 us -> 1.34 us
  starting transfers between devices: 12.3 us -> 0 us
  local copies, waits for them, and re-layouts: 17.3 us -> 5.99 us
  matrix products: 7.09 us -> 0 us
    psum x1 -> x0, waiting for transfers between devices: 75.7 us -> none  [per_device(): summed = lax.psum(partial_value, 'space')]
    pallas_call x0 -> x1, Pallas kernels: none -> 67.5 us  [per_device(): pl.pallas_call(lambda *refs: kernel(n, nt, *refs), out_shape=(jax.ShapeDt...]
    psum x1 -> x0, blocking collectives: 21.9 us -> none  [per_device(): correlator = lax.psum(spread, 'space')]
    ppermute x6 -> x0, waiting for transfers between devices: 20.9 us -> none  [shifted(): return lax.ppermute(block, axis, route)]
    ppermute x6 -> x0, starting transfers between devices: 12.3 us -> none  [shifted(): return lax.ppermute(block, axis, route)]
    reduce_sum x11 -> x0, other arithmetic: 10.4 us -> none  [the longest x10 6.87 us: contract(): return jnp.sum(matrix[:, :, :, None, :] * vector[:, None, :, :, :], axis=2)]
    all_gather x1 -> x0, waiting for transfers between devices: 9.91 us -> none  [per_device(): gathered = lax.all_gather(elemental[None], 'tm', axis=0, tiled=True)]
    another operation x34 -> x1, other arithmetic: 9.49 us -> 0.02 us  [per_device(): table = jnp.stack([jnp.cos(angle), jnp.sin(angle), pick, pick], axis=1)]
  transfers between devices with their start and end apart: 8 -> 0, of which waited for: 5 -> 0; matrix products, arithmetic and copies ran while one was open for 14% -> 0% of each run, Pallas kernels for 0% -> 0%
where the time goes in v1:
time: 79 us; the launch traced here: 77.6 us
  Pallas kernels  67.5 us (85%)
  local copies, waits for them, and re-layouts  5.99 us (8%)
  other arithmetic  2.77 us (4%)
  between operations  1.34 us (2%)
    pallas_call x1, Pallas kernels, per_device(): pl.pallas_call(lambda *refs: kernel(n, nt, *refs), out_shape=(jax.ShapeDt...  67.5 us
    unnamed x7, local copies, waits for them, and re-layouts  3.99 us

profile of v1, /device:TPU:0, one launch (start us, length us, event | category | flops | bytes accessed | tf_op | source)
XLA Modules:
  0.0 77.6 jit_solution(8210365362798935492)
XLA Ops:
  1.3 0.7 convert_element_type.30
  1.9 0.7 fusion.8
  2.6 0.6 multiply_multiply_fusion
  3.3 1.3 %fusion.3 = f32[128]{0:T(128)S(1)} fusion(f32[]{:T(128)} %bitcast.2, f32[]{:T(128)} %bitcast.1), kind=kLoop, calls=%fused_computation.9 | loop fusion | flops 2432 | bytes 520 | tf_op jit(solution)/shard_map/add | solution.py:471
  4.5 0.2 fusion.7
  4.7 0.1 sin.10
  4.9 0.8 copy.11
  5.7 0.0 copy-start
  5.7 1.6 %copy-done = bf16[1,8,2,256,256]{4,3,2,1,0:T(8,128)(2,1)S(1)} copy-done((bf16[1,8,2,256,256]{4,3,2,1,0:T(8,128)(2,1)S(1)}, bf16[1,8,2,256,256]{4,3,2,1,0:T(8,128)(2,1)}, u32[]{:S(2)}) %copy-start) | copy-done | bytes 2097176
  7.2 0.0 copy-start.1
  7.2 1.0 %copy-done.1 = bf16[1,2,1,3,256,128]{5,4,3,2,1,0:T(8,128)(2,1)S(1)} copy-done((bf16[1,2,1,3,256,128]{5,4,3,2,1,0:T(8,128)(2,1)S(1)}, bf16[1,2,1,3,256,128]{5,4,3,2,1,0:T(8,128)(2,1)}, u32[]{:S(2)}) %copy-start.1) | copy-done | bytes 393240
  8.2 0.0 copy-start.2
  8.2 0.7 copy-done.2
  8.9 67.5 %meson.1 = (bf16[32,512]{1,0:T(8,128)(2,1)S(1)}, f32[8,128]{1,0:T(8,128)S(1)}) custom-call(s32[4]{0:T(128)S(1)} %copy-done.2, bf16[6,8,32,128]{3,2,1,0:T(8,128)(2,1)S(1)} %bitcast.12, f32[18,3,128]{2,1,0:T(4,128)S(1)} %bitcast.13, f32[8,4,128]{2,1,0:T(4,128)S(1)} %pad_maximum_fusion.refs_3_, bf16[8,2,256,256]{3,2,1,0:T(8,128)(2,1)S(1)} %bitcast.11), custom_call_target="tpu_custom_call" | custom-call | tf_op jit(solution)/shard_map/meson/pallas_call | solution.py:485
  76.5 0.6 reshape.140
  77.1 0.6 slice.15
  (3 shorter events, 0.0 us)
Async XLA Ops:
  5.7 1.6 %copy-start = (bf16[1,8,2,256,256]{4,3,2,1,0:T(8,128)(2,1)S(1)}, bf16[1,8,2,256,256]{4,3,2,1,0:T(8,128)(2,1)}, u32[]{:S(2)}) copy-start(bf16[1,8,2,256,256]{4,3,2,1,0:T(8,128)(2,1)} %param.8) | copy-start | bytes 6291460
  7.2 1.0 %copy-start.1 = (bf16[1,2,1,3,256,128]{5,4,3,2,1,0:T(8,128)(2,1)S(1)}, bf16[1,2,1,3,256,128]{5,4,3,2,1,0:T(8,128)(2,1)}, u32[]{:S(2)}) copy-start(bf16[1,2,1,3,256,128]{5,4,3,2,1,0:T(8,128)(2,1)} %param.6) | copy-start | bytes 1179652
  8.2 0.7 copy-start.2

commit v2 on v1

--- a/solution.py
+++ b/solution.py
@@ -45,11 +45,11 @@
     return real + imag
 
 
+def rounded(field):
+    return [part.astype(jnp.bfloat16).astype(jnp.float32) for part in field]
+
+
 def apply_adjoint(link, field):
-    def flipped(part, i, j):
-        value = link(part, j, i)
-        return value if part == 0 else -value
-
     real = []
     imag = []
     for i in range(3):
@@ -86,16 +86,16 @@
     n,
     nt,
     source_ref,
+    direction_ref,
+    momentum_ref,
     field_ref,
     gauge_ref,
-    table_ref,
     block_ref,
     own_ref,
     trace_ref,
     gauge_own,
-    gauge_send,
-    gauge_in,
     gauge_all,
+    table,
     field_in,
     once,
     twice,
@@ -105,7 +105,7 @@
     part_send,
     part_in,
     own_send,
-    rows_tm,
+    rows_all,
     rows_sink,
     source_send,
     rows_source,
@@ -118,9 +118,13 @@
     tm_send_sem,
     tm_recv_sem,
     block_sem,
+    local_sem,
 ):
     me = lax.axis_index("space")
     tm_me = lax.axis_index("tm")
+    per = n // nt
+    layer = me // per
+    member = tm_me * per + lax.rem(me, per)
     rows = field_ref.shape[2]
     chunk = row_chunk(rows)
     per_plane = rows // chunk
@@ -130,87 +134,155 @@
     load_blocks = pltpu.make_async_copy(block_ref, blocks, block_sem)
     load_blocks.start()
 
+    def member_id(which, index):
+        return {"tm": index // per, "space": which * per + lax.rem(index, per)}
+
+    def each_peer(act, mine=member, lead=1):
+        def step(d, carry):
+            act(lax.rem(mine + d, n))
+            return carry
+
+        lax.fori_loop(lead, n, step, 0)
+
+    def each_layer(act):
+        def step(d, carry):
+            act(lax.rem(layer + d, nt))
+            return carry
+
+        lax.fori_loop(1, nt, step, 0)
+
+    def is_self(device):
+        return jnp.logical_and(device["tm"] == tm_me, device["space"] == me)
+
     barrier = pltpu.get_barrier_semaphore()
 
-    def greet_space(d, carry):
-        pl.semaphore_signal(
-            barrier, inc=1, device_id={"space": lax.rem(me + d, n)}, device_id_type=MESH
-        )
-        return carry
-
-    def greet_tm(d, carry):
-        pl.semaphore_signal(
-            barrier, inc=1, device_id={"tm": lax.rem(tm_me + d, nt)}, device_id_type=MESH
-        )
-        return carry
-
-    lax.fori_loop(1, n, greet_space, 0)
-    lax.fori_loop(1, nt, greet_tm, 0)
-
-    for k in range(gauge_ref.shape[0]):
-        gauge_own[pl.ds(3 * k, 3), :] = gauge_ref[k]
-    gauge_send[...] = gauge_own[...].astype(jnp.bfloat16)
-    gauge_in[me] = gauge_send[...]
-    field_in[me] = field_ref[:, me]
-    pl.semaphore_wait(barrier, n - 1 + nt - 1)
-
-    def remote(kind, source, target, peer, slot):
+    def greet(device):
+        pl.semaphore_signal(barrier, inc=1, device_id=device, device_id_type=MESH)
+
+    def greet_origin(plane):
+        origin = {"tm": layer, "space": plane}
+
+        @pl.when(jnp.logical_not(is_self(origin)))
+        def _():
+            greet(origin)
+
+    each_peer(greet_origin, lead=0)
+    each_peer(lambda index: greet(member_id(layer, index)))
+    each_peer(lambda index: greet({"tm": tm_me, "space": index}), mine=me)
+    each_layer(lambda index: greet(member_id(index, member)))
+
+    for k in range(54):
+        gauge_own[pl.ds(k, 1), :] = gauge_ref[k]
+    towards = direction_ref[0].astype(jnp.float32)
+    gauge_own[pl.ds(54, 2), :] = jnp.full((2, lanes), towards, jnp.float32)
+    at_home = jnp.where(layer == tm_me, 1, 0)
+    pl.semaphore_wait(barrier, n - at_home + n - 1 + n - 1 + nt - 1)
+
+    def remote(kind, source, target, device, peer, slot):
         return pltpu.make_async_remote_copy(
             src_ref=source,
             dst_ref=target,
             send_sem=send_sem.at[kind, peer],
             recv_sem=recv_sem.at[kind, slot],
-            device_id={"space": peer},
+            device_id=device,
             device_id_type=MESH,
         )
 
-    def each_peer(act):
-        def step(d, carry):
-            act(lax.rem(me + d, n))
-            return carry
-
-        lax.fori_loop(1, n, step, 0)
-
-    def gauge_copy(peer, slot):
-        return remote(0, gauge_send, gauge_in.at[slot], peer, slot)
-
-    def field_copy(peer, slot):
-        return remote(1, field_ref.at[:, peer], field_in.at[slot], peer, slot)
+    def gauge_copy(device, peer, slot):
+        return remote(0, gauge_own, gauge_all.at[slot], device, peer, slot)
+
+    def field_copy(device, peer, slot):
+        return remote(1, field_ref.at[:, peer], field_in.at[slot], device, peer, slot)
+
+    def home_copy():
+        return pltpu.make_async_copy(field_ref.at[:, member], field_in.at[me], local_sem)
 
     def twice_copy(peer, slot):
-        return remote(2, twice.at[peer], twice_in.at[slot], peer, slot)
+        return remote(2, twice.at[peer], twice_in.at[slot], member_id(layer, peer), peer, slot)
 
     def gradient_copy(peer, slot):
-        return remote(3, gradient.at[peer], gradient_in.at[slot], peer, slot)
+        return remote(
+            3, gradient.at[peer], gradient_in.at[slot], member_id(layer, peer), peer, slot
+        )
 
     def part_copy(peer, slot):
-        return remote(4, part_send.at[peer], part_in.at[slot], peer, slot)
+        return remote(4, part_send.at[peer], part_in.at[slot], member_id(layer, peer), peer, slot)
 
     def sink_copy(peer, slot):
-        return remote(5, own_send, rows_sink.at[slot], peer, slot)
+        return remote(
+            5, rows_all.at[peer // per], rows_sink.at[slot], member_id(layer, peer), peer, slot
+        )
 
     def source_copy(peer, slot):
-        return remote(6, source_send.at[peer], rows_source.at[slot], peer, slot)
+        return remote(6, source_send, rows_source.at[slot], member_id(layer, peer), peer, slot)
 
     def trace_copy(peer, slot):
-        return remote(7, trace_send, trace_in.at[slot], peer, slot)
-
-    def start_all(copy):
-        each_peer(lambda peer: copy(peer, me).start())
-
-    def arrive_all(copy):
-        each_peer(lambda peer: copy(peer, peer).wait_recv())
-
-    start_all(gauge_copy)
-    start_all(field_copy)
-    arrive_all(gauge_copy)
-
-    def widen(z, carry):
-        gauge_all[z] = gauge_in[z].astype(jnp.float32)
-        return carry
-
-    lax.fori_loop(0, n, widen, 0)
-    arrive_all(field_copy)
+        return remote(
+            7, trace_send, trace_in.at[slot], {"tm": tm_me, "space": peer}, peer, slot
+        )
+
+    def start_all(copy, mine=member):
+        each_peer(lambda peer: copy(peer, mine).start(), mine=mine)
+
+    def arrive_all(copy, mine=member):
+        each_peer(lambda peer: copy(peer, peer).wait_recv(), mine=mine)
+
+    def send_gauge(peer):
+        device = member_id(tm_me, peer)
+
+        @pl.when(jnp.logical_not(is_self(device)))
+        def _():
+            gauge_copy(device, peer, me).start()
+
+    def send_field(peer):
+        device = member_id(tm_me, peer)
+
+        @pl.when(jnp.logical_not(is_self(device)))
+        def _():
+            field_copy(device, peer, me).start()
+
+    each_peer(send_gauge, lead=0)
+    each_peer(send_field, lead=0)
+
+    @pl.when(layer == tm_me)
+    def _():
+        home_copy().start()
+        gauge_all[me] = gauge_own[...]
+
+    plane_at = lax.broadcasted_iota(jnp.int32, (n, lanes), 0).astype(jnp.float32)
+    site = lax.broadcasted_iota(jnp.int32, (n, lanes), 1)
+    angle = (
+        2.0
+        * math.pi
+        * (
+            momentum_ref[0].astype(jnp.float32) * (site % SX).astype(jnp.float32) / SX
+            + momentum_ref[1].astype(jnp.float32) * (site // SX).astype(jnp.float32) / SY
+            + momentum_ref[2].astype(jnp.float32) * plane_at / n
+        )
+    )
+    table[0] = jnp.cos(angle)
+    table[1] = jnp.sin(angle)
+
+    def take_gauge(plane):
+        origin = {"tm": layer, "space": plane}
+
+        @pl.when(jnp.logical_not(is_self(origin)))
+        def _():
+            gauge_copy(member_id(tm_me, lax.rem(member + 1, n)), plane, plane).wait_recv()
+
+    def take_field(plane):
+        origin = {"tm": layer, "space": plane}
+        mine = is_self(origin)
+
+        @pl.when(jnp.logical_not(mine))
+        def _():
+            field_copy(member_id(tm_me, lax.rem(member + 1, n)), plane, plane).wait_recv()
+
+        @pl.when(mine)
+        def _():
+            home_copy().wait()
+
+    each_peer(take_gauge, lead=0)
 
     column = lax.broadcasted_iota(jnp.int32, (chunk, lanes), 1) % SX
 
@@ -240,7 +312,7 @@
         add(apply_link(link_at(z, 1), [ahead_y(part) for part in here]))
         add([behind_y(part) for part in apply_adjoint(link_at(z, 1), here)])
         add(apply_link(link_at(z, 2), field_at(above)))
-        add(apply_adjoint(link_at(below, 2), field_at(below)))
+        add(rounded(apply_adjoint(link_at(below, 2), field_at(below))))
         for k in range(6):
             out[z, k, span, :] = (here[k] + smear_kappa * total[k]).astype(jnp.bfloat16)
 
@@ -252,7 +324,7 @@
         def field_at(plane):
             return [twice[plane, k, span, :].astype(jnp.float32) for k in range(6)]
 
-        pick = table_ref[z, pl.ds(2, 1), :]
+        pick = gauge_all[z, pl.ds(54, 1), :]
         along_x = pick == 0.0
         along_y = pick == 1.0
         along_z = pick == 2.0
@@ -289,12 +361,12 @@
         forward = apply_link(chosen, incoming)
         back = apply_adjoint(chosen_back, base)
         back = [
-            jnp.where(wide_x, behind_x(part, column), jnp.where(wide_y, behind_y(part), part))
-            for part in back
+            jnp.where(wide_x, behind_x(part, column), jnp.where(wide_y, behind_y(part), carried))
+            for part, carried in zip(back, rounded(back))
         ]
         slope = [forward[k] - back[k] for k in range(6)]
-        cosine = table_ref[z, pl.ds(0, 1), :]
-        sine = table_ref[z, pl.ds(1, 1), :]
+        cosine = table[0, pl.ds(z, 1), :]
+        sine = table[1, pl.ds(z, 1), :]
         for c in range(3):
             real, imag = slope[c], slope[3 + c]
             gradient[z, c, span, :] = (cosine * real + sine * imag).astype(jnp.bfloat16)
@@ -307,40 +379,51 @@
 
         lax.fori_loop(0, per_plane, step, 0)
 
-    bufs = [field_in, once, twice]
-    for sweep_index in range(SMEAR - 1):
-
-        def sweep_plane(z, carry):
-            each_piece(lambda piece: sweep(bufs[0], bufs[1], z, piece))
-            return carry
-
-        lax.fori_loop(0, n, sweep_plane, 0)
+    turn = jnp.where(2 * layer < nt, 1, -1)
+    begin = jnp.where(2 * layer < nt, layer * per + 1, layer * per)
+
+    def first_plane(d, carry):
+        z = lax.rem(begin + turn * d + n, n)
+
+        @pl.when(d == 0)
+        def _():
+            take_field(lax.rem(z - turn + n, n))
+            take_field(z)
+
+        @pl.when(d < n - 2)
+        def _():
+            take_field(lax.rem(z + turn + n, n))
+
+        each_piece(lambda piece: sweep(field_in, once, z, piece))
+        return carry
+
+    lax.fori_loop(0, n, first_plane, 0)
 
     def last_plane(d, carry):
-        z = lax.rem(me + d, n)
+        z = lax.rem(member + d, n)
         each_piece(lambda piece: sweep(once, twice, z, piece))
 
         @pl.when(d < n)
         def _():
-            twice_copy(z, me).start()
+            twice_copy(z, member).start()
 
         return carry
 
     lax.fori_loop(1, n + 1, last_plane, 0)
-    twice_in[me] = twice[me]
+    twice_in[member] = twice[member]
 
     def derive_plane(d, carry):
-        z = lax.rem(me + d, n)
+        z = lax.rem(member + d, n)
         each_piece(lambda piece: derive(z, piece))
 
         @pl.when(d < n)
         def _():
-            gradient_copy(z, me).start()
+            gradient_copy(z, member).start()
 
         return carry
 
     lax.fori_loop(1, n + 1, derive_plane, 0)
-    gradient_in[me] = gradient[me]
+    gradient_in[member] = gradient[member]
 
     arrive_all(twice_copy)
     arrive_all(gradient_copy)
@@ -353,48 +436,38 @@
     sum_imag = lax.dot_general(left, right_imag, nt_dims, preferred_element_type=jnp.float32)
     part_send[:, :, :nv] = sum_real.reshape(n, rows, nv).astype(jnp.bfloat16)
     part_send[:, :, nv:] = sum_imag.reshape(n, rows, nv).astype(jnp.bfloat16)
-    part_in[me] = part_send[me]
+    part_in[member] = part_send[member]
     start_all(part_copy)
     arrive_all(part_copy)
     scale = 1.0 / math.sqrt(3 * SX * SY * n)
     summed = jnp.sum(part_in[...].astype(jnp.float32), axis=0)
     own = (summed * scale).astype(jnp.bfloat16)
     own_send[...] = own
-    own_ref[...] = own
-    rows_sink[me] = own
-    rows_tm[tm_me] = own
-
-    def tm_copy(peer, slot):
+    rows_all[layer] = own
+
+    def layer_copy(peer, slot):
         return pltpu.make_async_remote_copy(
             src_ref=own_send,
-            dst_ref=rows_tm.at[slot],
+            dst_ref=rows_all.at[slot],
             send_sem=tm_send_sem.at[peer],
             recv_sem=tm_recv_sem.at[slot],
-            device_id={"tm": peer},
+            device_id=member_id(peer, member),
             device_id_type=MESH,
         )
 
-    def each_tm(act):
-        def step(d, carry):
-            act(lax.rem(tm_me + d, nt))
-            return carry
-
-        lax.fori_loop(1, nt, step, 0)
-
-    each_tm(lambda peer: tm_copy(peer, tm_me).start())
+    each_layer(lambda peer: layer_copy(peer, layer).start())
+    each_layer(lambda peer: layer_copy(peer, peer).wait_recv())
     start_all(sink_copy)
-    each_tm(lambda peer: tm_copy(peer, peer).wait_recv())
-
-    def fill_source(i, carry):
-        source_send[i] = rows_tm[source_ref[i // (n // nt)]]
-        return carry
-
-    lax.fori_loop(0, n, fill_source, 0)
-    rows_source[me] = source_send[me]
+    source_send[...] = rows_all[source_ref[layer]]
     start_all(source_copy)
+    rows_sink[member] = rows_all[tm_me]
+    rows_source[member] = source_send[...]
     arrive_all(sink_copy)
     load_blocks.wait()
 
+    mine_rows = rows_sink[me].astype(jnp.float32)
+    own_ref[:, 0, :] = mine_rows[:, :nv].astype(jnp.bfloat16)
+    own_ref[:, 1, :] = mine_rows[:, nv:].astype(jnp.bfloat16)
     sink = flat_rows(rows_sink[...])
     weight[...] = jnp.zeros_like(weight)
 
@@ -430,27 +503,30 @@
     trace_imag = jnp.sum(partner_real * weight_imag + partner_imag * weight_real)
     row = lax.broadcasted_iota(jnp.int32, trace_send.shape, 0)
     lane = lax.broadcasted_iota(jnp.int32, trace_send.shape, 1)
-    mine = source_ref[me // (n // nt)]
+    mine = source_ref[layer]
     value = jnp.where(row == 0, trace_real, jnp.where(row == 1, trace_imag, 0.0))
     value = jnp.where(lane == mine, value, 0.0) * (1.0 / (NS * nv))
     trace_send[...] = value
     trace_in[me] = value
-    start_all(trace_copy)
-    arrive_all(trace_copy)
-    trace_ref[...] = jnp.sum(trace_in[...], axis=0)
-
-    for copy in (
-        gauge_copy,
-        field_copy,
-        twice_copy,
-        gradient_copy,
-        part_copy,
-        sink_copy,
-        source_copy,
-        trace_copy,
-    ):
-        each_peer(lambda peer: copy(peer, me).wait_send())
-    each_tm(lambda peer: tm_copy(peer, tm_me).wait_send())
+    start_all(trace_copy, mine=me)
+    arrive_all(trace_copy, mine=me)
+    total = jnp.sum(trace_in[...], axis=0)
+    trace_ref[0] = total[0:1, :nt]
+    trace_ref[1] = total[1:2, :nt]
+
+    def sent_first(peer):
+        device = member_id(tm_me, peer)
+
+        @pl.when(jnp.logical_not(is_self(device)))
+        def _():
+            gauge_copy(device, peer, me).wait_send()
+            field_copy(device, peer, me).wait_send()
+
+    each_peer(sent_first, lead=0)
+    for copy in (twice_copy, gradient_copy, part_copy, sink_copy, source_copy):
+        each_peer(lambda peer: copy(peer, member).wait_send())
+    each_peer(lambda peer: trace_copy(peer, me).wait_send(), mine=me)
+    each_layer(lambda peer: layer_copy(peer, layer).wait_send())
 
 
 def per_device(n, nt, vectors, gauge_links, perambulator, directions, momentum, source_list):
@@ -458,43 +534,27 @@
     lanes = vectors.shape[5]
     rows = nv // n
     field = vectors.reshape(6, n, rows, lanes)
-    gauge = gauge_links.reshape(18, 3, lanes)
+    gauge = gauge_links.reshape(54, 1, lanes)
     block_set = perambulator[0]
-
-    site = jnp.arange(lanes)
-    moment = momentum.astype(jnp.float32)
-    plane = jnp.arange(n).astype(jnp.float32)
-    angle = (
-        2.0
-        * math.pi
-        * (
-            moment[0] * (site % SX).astype(jnp.float32)[None, :] / SX
-            + moment[1] * (site // SX).astype(jnp.float32)[None, :] / SY
-            + moment[2] * plane[:, None] / n
-        )
-    )
-    pick = jnp.broadcast_to(directions[0].astype(jnp.float32), angle.shape)
-    table = jnp.stack([jnp.cos(angle), jnp.sin(angle), pick, pick], axis=1)
 
     bf16, f32 = jnp.bfloat16, jnp.float32
     vmem = pl.BlockSpec(memory_space=pltpu.VMEM)
     smem = pl.BlockSpec(memory_space=pltpu.SMEM)
-    anywhere = pl.BlockSpec(memory_space=pl.ANY)
+    anywhere = pl.BlockSpec(memory_space=pltpu.HBM)
     split = (n, 6, rows, lanes)
     count = block_set.shape[0]
     own, trace = pl.pallas_call(
         lambda *refs: kernel(n, nt, *refs),
         out_shape=(
-            jax.ShapeDtypeStruct((rows, 2 * nv), bf16),
-            jax.ShapeDtypeStruct((8, 128), f32),
+            jax.ShapeDtypeStruct((rows, 2, nv), bf16),
+            jax.ShapeDtypeStruct((2, 1, nt), f32),
         ),
-        in_specs=[smem, vmem, vmem, vmem, anywhere],
+        in_specs=[smem, smem, smem, anywhere, vmem, anywhere],
         out_specs=(vmem, vmem),
         scratch_shapes=[
-            pltpu.VMEM((64, lanes), f32),
-            pltpu.VMEM((64, lanes), bf16),
-            pltpu.VMEM((n, 64, lanes), bf16),
-            pltpu.VMEM((n, 64, lanes), f32),
+            pltpu.VMEM((56, lanes), f32),
+            pltpu.VMEM((n, 56, lanes), f32),
+            pltpu.VMEM((2, n, lanes), f32),
             pltpu.VMEM(split, bf16),
             pltpu.VMEM(split, bf16),
             pltpu.VMEM(split, bf16),
@@ -506,7 +566,7 @@
             pltpu.VMEM((rows, 2 * nv), bf16),
             pltpu.VMEM((nt, rows, 2 * nv), bf16),
             pltpu.VMEM((n, rows, 2 * nv), bf16),
-            pltpu.VMEM((n, rows, 2 * nv), bf16),
+            pltpu.VMEM((rows, 2 * nv), bf16),
             pltpu.VMEM((n, rows, 2 * nv), bf16),
             pltpu.VMEM((count, 2, nv, nv), bf16),
             pltpu.VMEM((nv, 2 * nv), f32),
@@ -517,13 +577,14 @@
             pltpu.SemaphoreType.DMA((nt,)),
             pltpu.SemaphoreType.DMA((nt,)),
             pltpu.SemaphoreType.DMA,
+            pltpu.SemaphoreType.DMA,
         ],
         compiler_params=pltpu.CompilerParams(
             collective_id=0, has_side_effects=True, vmem_limit_bytes=40 * 1024 * 1024
         ),
         name="meson",
-    )(source_list, field, gauge, table, block_set)
-    return (own.reshape(1, rows, 2, nv), trace[:2, None, :nt])
+    )(source_list, directions, momentum, field, gauge, block_set)
+    return (own[None], trace)
 
 
 def solution(mesh):

time: 79 us -> 80.4 us (1.018); the launches traced: 77.6 us -> 80 us
  Pallas kernels: 67.5 us -> 72.9 us
  other arithmetic: 2.77 us -> 0 us
    pallas_call x1, Pallas kernels: 67.5 us -> 72.9 us  [per_device(): pl.pallas_call(lambda *refs: kernel(n, nt, *refs), out_shape=(jax.ShapeDt...]
    unnamed x7 -> x12, local copies, waits for them, and re-layouts: 3.99 us -> 5.81 us
    add x1 -> x0, other arithmetic: 1.25 us -> none  [per_device(): moment[0] * (site % SX).astype(jnp.float32)[None, :] / SX]
    slice x2 -> x0, local copies, waits for them, and re-layouts: 1.23 us -> none  [the longest x1 0.67 us: per_device(): moment[2] * plane[:, None] / n]
where the time goes in v2:
time: 80.4 us; the launch traced here: 80 us
  Pallas kernels  72.9 us (91%)
  local copies, waits for them, and re-layouts  5.81 us (7%)
  between operations  1.3 us (2%)
    pallas_call x1, Pallas kernels, per_device(): pl.pallas_call(lambda *refs: kernel(n, nt, *refs), out_shape=(jax.ShapeDt...  72.9 us
    unnamed x12, local copies, waits for them, and re-layouts  5.81 us

profile of v2, /device:TPU:0, one launch (start us, length us, event | category | flops | bytes accessed | tf_op | source)
XLA Modules:
  0.0 80.0 jit_solution(3192602549144370894)
XLA Ops:
  1.3 0.0 copy-start
  1.3 1.6 %copy-done = bf16[1,8,2,256,256]{4,3,2,1,0:T(8,128)(2,1)S(1)} copy-done((bf16[1,8,2,256,256]{4,3,2,1,0:T(8,128)(2,1)S(1)}, bf16[1,8,2,256,256]{4,3,2,1,0:T(8,128)(2,1)}, u32[]{:S(2)}) %copy-start) | copy-done | bytes 2097176
  2.9 0.0 copy-start.1
  2.9 1.0 %copy-done.1 = bf16[1,2,1,3,256,128]{5,4,3,2,1,0:T(8,128)(2,1)S(1)} copy-done((bf16[1,2,1,3,256,128]{5,4,3,2,1,0:T(8,128)(2,1)S(1)}, bf16[1,2,1,3,256,128]{5,4,3,2,1,0:T(8,128)(2,1)}, u32[]{:S(2)}) %copy-start.1) | copy-done | bytes 393240
  3.9 0.0 copy-start.2
  3.9 0.7 copy-done.2
  4.6 0.0 copy-start.3
  4.6 0.7 copy-done.3
  5.3 0.0 copy-start.4
  5.3 0.7 copy-done.4
  5.9 72.9 %meson.1 = (bf16[32,2,256]{2,1,0:T(2,128)(2,1)S(1)}, f32[2,1,4]{2,1,0:T(1,128)S(1)}) custom-call(s32[4]{0:T(128)S(1)} %copy-done.3, s32[1]{0:T(128)S(6)} %copy.10.refs_1_, s32[3]{0:T(128)S(1)} %copy-done.4, bf16[6,8,32,128]{3,2,1,0:T(8,128)(2,1)S(1)} %bitcast.5, f32[54,1,128]{2,1,0:T(1,128)S(1)} %bitcast.7, bf16[8,2,256,256]{3,2,1,0:T(8,128)(2,1)S(1)} %bitcast.4), custom_call_target="tpu_custom_call" | custom-call | tf_op jit(solution)/shard_map/meson/pallas_call | solution.py:546
  78.8 0.6 copy.11
  79.4 0.6 copy.12
Async XLA Ops:
  1.3 1.6 %copy-start = (bf16[1,8,2,256,256]{4,3,2,1,0:T(8,128)(2,1)S(1)}, bf16[1,8,2,256,256]{4,3,2,1,0:T(8,128)(2,1)}, u32[]{:S(2)}) copy-start(bf16[1,8,2,256,256]{4,3,2,1,0:T(8,128)(2,1)} %param.8) | copy-start | bytes 6291460
  2.9 1.0 %copy-start.1 = (bf16[1,2,1,3,256,128]{5,4,3,2,1,0:T(8,128)(2,1)S(1)}, bf16[1,2,1,3,256,128]{5,4,3,2,1,0:T(8,128)(2,1)}, u32[]{:S(2)}) copy-start(bf16[1,2,1,3,256,128]{5,4,3,2,1,0:T(8,128)(2,1)} %param.6) | copy-start | bytes 1179652
  3.9 0.7 copy-start.2
  4.6 0.7 copy-start.3
  5.3 0.7 copy-start.4

commit v3 on v2

--- a/solution.py
+++ b/solution.py
@@ -95,6 +95,7 @@
     trace_ref,
     gauge_own,
     gauge_all,
+    gauge_wide,
     table,
     field_in,
     once,
@@ -110,7 +111,8 @@
     source_send,
     rows_source,
     blocks,
-    weight,
+    firsts,
+    right_side,
     trace_send,
     trace_in,
     send_sem,
@@ -166,17 +168,25 @@
         def _():
             greet(origin)
 
+    def greet_target(index):
+        target = member_id(tm_me, index)
+
+        @pl.when(jnp.logical_not(is_self(target)))
+        def _():
+            greet(target)
+
     each_peer(greet_origin, lead=0)
+    each_peer(greet_target, lead=0)
     each_peer(lambda index: greet(member_id(layer, index)))
     each_peer(lambda index: greet({"tm": tm_me, "space": index}), mine=me)
     each_layer(lambda index: greet(member_id(index, member)))
 
     for k in range(54):
-        gauge_own[pl.ds(k, 1), :] = gauge_ref[k]
+        gauge_own[k] = gauge_ref[k]
     towards = direction_ref[0].astype(jnp.float32)
-    gauge_own[pl.ds(54, 2), :] = jnp.full((2, lanes), towards, jnp.float32)
+    gauge_own[54] = jnp.full((1, lanes), towards, jnp.float32)
     at_home = jnp.where(layer == tm_me, 1, 0)
-    pl.semaphore_wait(barrier, n - at_home + n - 1 + n - 1 + nt - 1)
+    pl.semaphore_wait(barrier, 2 * (n - at_home) + n - 1 + n - 1 + nt - 1)
 
     def remote(kind, source, target, device, peer, slot):
         return pltpu.make_async_remote_copy(
@@ -208,10 +218,8 @@
     def part_copy(peer, slot):
         return remote(4, part_send.at[peer], part_in.at[slot], member_id(layer, peer), peer, slot)
 
-    def sink_copy(peer, slot):
-        return remote(
-            5, rows_all.at[peer // per], rows_sink.at[slot], member_id(layer, peer), peer, slot
-        )
+    def sink_copy(device, peer, slot):
+        return remote(5, own_send, rows_sink.at[slot], device, peer, slot)
 
     def source_copy(peer, slot):
         return remote(6, source_send, rows_source.at[slot], member_id(layer, peer), peer, slot)
@@ -284,11 +292,19 @@
 
     each_peer(take_gauge, lead=0)
 
+    def widen(z, carry):
+        for k in range(54):
+            gauge_wide[z, k] = jnp.broadcast_to(gauge_all[z, k], (8, lanes))
+        return carry
+
+    lax.fori_loop(0, n, widen, 0)
+
     column = lax.broadcasted_iota(jnp.int32, (chunk, lanes), 1) % SX
 
     def link_at(z, direction):
         def link(part, i, j):
-            return gauge_all[z, pl.ds(((direction * 2 + part) * 3 + i) * 3 + j, 1), :]
+            tile = gauge_wide[z, ((direction * 2 + part) * 3 + i) * 3 + j]
+            return jnp.concatenate([tile] * (chunk // 8), axis=0)
 
         return link
 
@@ -324,28 +340,25 @@
         def field_at(plane):
             return [twice[plane, k, span, :].astype(jnp.float32) for k in range(6)]
 
-        pick = gauge_all[z, pl.ds(54, 1), :]
-        along_x = pick == 0.0
-        along_y = pick == 1.0
-        along_z = pick == 2.0
-        wide_x = jnp.broadcast_to(pick, (chunk, lanes)) == 0.0
-        wide_y = jnp.broadcast_to(pick, (chunk, lanes)) == 1.0
-        wide_z = jnp.broadcast_to(pick, (chunk, lanes)) == 2.0
+        pick = jnp.broadcast_to(gauge_all[z, 54], (chunk, lanes))
+        wide_x = pick == 0.0
+        wide_y = pick == 1.0
+        wide_z = pick == 2.0
         links = [link_at(z, direction) for direction in range(3)]
         link_below = link_at(below, 2)
 
         def chosen(part, i, j):
             return jnp.where(
-                along_x,
+                wide_x,
                 links[0](part, i, j),
-                jnp.where(along_y, links[1](part, i, j), links[2](part, i, j)),
+                jnp.where(wide_y, links[1](part, i, j), links[2](part, i, j)),
             )
 
         def chosen_back(part, i, j):
             return jnp.where(
-                along_x,
+                wide_x,
                 links[0](part, i, j),
-                jnp.where(along_y, links[1](part, i, j), link_below(part, i, j)),
+                jnp.where(wide_y, links[1](part, i, j), link_below(part, i, j)),
             )
 
         here = field_at(z)
@@ -455,52 +468,78 @@
             device_id_type=MESH,
         )
 
+    def send_sink(plane):
+        device = {"tm": layer, "space": plane}
+
+        @pl.when(jnp.logical_not(is_self(device)))
+        def _():
+            sink_copy(device, plane, member).start()
+
+    def take_sink(index):
+        origin = member_id(tm_me, index)
+
+        @pl.when(jnp.logical_not(is_self(origin)))
+        def _():
+            sink_copy({"tm": tm_me, "space": lax.rem(me + 1, n)}, index, index).wait_recv()
+
     each_layer(lambda peer: layer_copy(peer, layer).start())
+    each_peer(send_sink, mine=me, lead=0)
+
+    @pl.when(layer == tm_me)
+    def _():
+        rows_sink[member] = own_send[...]
+
     each_layer(lambda peer: layer_copy(peer, peer).wait_recv())
-    start_all(sink_copy)
     source_send[...] = rows_all[source_ref[layer]]
     start_all(source_copy)
-    rows_sink[member] = rows_all[tm_me]
     rows_source[member] = source_send[...]
-    arrive_all(sink_copy)
+    each_peer(take_sink, lead=0)
     load_blocks.wait()
 
     mine_rows = rows_sink[me].astype(jnp.float32)
     own_ref[:, 0, :] = mine_rows[:, :nv].astype(jnp.bfloat16)
     own_ref[:, 1, :] = mine_rows[:, nv:].astype(jnp.bfloat16)
     sink = flat_rows(rows_sink[...])
-    weight[...] = jnp.zeros_like(weight)
-
-    def one_block(q, carry):
+
+    def first_block(q, carry):
         real = blocks[q, 0]
         imag = blocks[q, 1]
         tall = jnp.concatenate([real, -imag], axis=0)
         tall_imag = jnp.concatenate([imag, real], axis=0)
-        first_real = jnp.dot(sink, tall, preferred_element_type=jnp.float32)
-        first_imag = jnp.dot(sink, tall_imag, preferred_element_type=jnp.float32)
-        stacked = jnp.concatenate([first_real, first_imag], axis=0).astype(jnp.bfloat16)
-        tn_dims = (((0,), (0,)), ((), ()))
-        weight[:, :nv] += lax.dot_general(
-            stacked,
-            jnp.concatenate([real, imag], axis=0),
-            tn_dims,
-            preferred_element_type=jnp.float32,
+        firsts[q, :, :nv] = jnp.dot(sink, tall, preferred_element_type=jnp.float32).astype(
+            jnp.bfloat16
         )
-        weight[:, nv:] += lax.dot_general(
-            stacked,
-            jnp.concatenate([-imag, real], axis=0),
-            tn_dims,
-            preferred_element_type=jnp.float32,
+        firsts[q, :, nv:] = jnp.dot(sink, tall_imag, preferred_element_type=jnp.float32).astype(
+            jnp.bfloat16
         )
         return carry
 
-    lax.fori_loop(0, blocks.shape[0], one_block, 0)
+    lax.fori_loop(0, blocks.shape[0], first_block, 0)
     arrive_all(source_copy)
-    partner = flat_rows(rows_source[...]).astype(jnp.float32)
+    partner = flat_rows(rows_source[...])
     partner_real, partner_imag = partner[:, :nv], partner[:, nv:]
-    weight_real, weight_imag = weight[:, :nv], weight[:, nv:]
-    trace_real = jnp.sum(partner_real * weight_real - partner_imag * weight_imag)
-    trace_imag = jnp.sum(partner_real * weight_imag + partner_imag * weight_real)
+    right_side[:nv, :nv] = partner_real
+    right_side[:nv, nv:] = partner_imag
+    right_side[nv:, :nv] = -partner_imag
+    right_side[nv:, nv:] = partner_real
+
+    def fold(values):
+        return jnp.sum(values.reshape(nv // 8, 8, nv), axis=0)
+
+    def second_block(q, carry):
+        sum_real, sum_imag = carry
+        second = jnp.dot(firsts[q], right_side[...], preferred_element_type=jnp.float32)
+        second_real, second_imag = second[:, :nv], second[:, nv:]
+        real = blocks[q, 0].astype(jnp.float32)
+        imag = blocks[q, 1].astype(jnp.float32)
+        sum_real = sum_real + fold(second_real * real + second_imag * imag)
+        sum_imag = sum_imag + fold(second_imag * real - second_real * imag)
+        return sum_real, sum_imag
+
+    nothing = jnp.zeros((8, nv), jnp.float32)
+    sum_real, sum_imag = lax.fori_loop(0, blocks.shape[0], second_block, (nothing, nothing))
+    trace_real = jnp.sum(sum_real)
+    trace_imag = jnp.sum(sum_imag)
     row = lax.broadcasted_iota(jnp.int32, trace_send.shape, 0)
     lane = lax.broadcasted_iota(jnp.int32, trace_send.shape, 1)
     mine = source_ref[layer]
@@ -523,7 +562,15 @@
             field_copy(device, peer, me).wait_send()
 
     each_peer(sent_first, lead=0)
-    for copy in (twice_copy, gradient_copy, part_copy, sink_copy, source_copy):
+    def sent_sink(plane):
+        device = {"tm": layer, "space": plane}
+
+        @pl.when(jnp.logical_not(is_self(device)))
+        def _():
+            sink_copy(device, plane, member).wait_send()
+
+    each_peer(sent_sink, mine=me, lead=0)
+    for copy in (twice_copy, gradient_copy, part_copy, source_copy):
         each_peer(lambda peer: copy(peer, member).wait_send())
     each_peer(lambda peer: trace_copy(peer, me).wait_send(), mine=me)
     each_layer(lambda peer: layer_copy(peer, layer).wait_send())
@@ -552,8 +599,9 @@
         in_specs=[smem, smem, smem, anywhere, vmem, anywhere],
         out_specs=(vmem, vmem),
         scratch_shapes=[
-            pltpu.VMEM((56, lanes), f32),
-            pltpu.VMEM((n, 56, lanes), f32),
+            pltpu.VMEM((55, 1, lanes), f32),
+            pltpu.VMEM((n, 55, 1, lanes), f32),
+            pltpu.VMEM((n, 54, 8, lanes), f32),
             pltpu.VMEM((2, n, lanes), f32),
             pltpu.VMEM(split, bf16),
             pltpu.VMEM(split, bf16),
@@ -569,7 +617,8 @@
             pltpu.VMEM((rows, 2 * nv), bf16),
             pltpu.VMEM((n, rows, 2 * nv), bf16),
             pltpu.VMEM((count, 2, nv, nv), bf16),
-            pltpu.VMEM((nv, 2 * nv), f32),
+            pltpu.VMEM((count, nv, 2 * nv), bf16),
+            pltpu.VMEM((2 * nv, 2 * nv), bf16),
             pltpu.VMEM((8, 128), f32),
             pltpu.VMEM((n, 8, 128), f32),
             pltpu.SemaphoreType.DMA((8, n)),
@@ -580,7 +629,7 @@
             pltpu.SemaphoreType.DMA,
         ],
         compiler_params=pltpu.CompilerParams(
-            collective_id=0, has_side_effects=True, vmem_limit_bytes=40 * 1024 * 1024
+            collective_id=0, has_side_effects=True, vmem_limit_bytes=60 * 1024 * 1024
         ),
         name="meson",
     )(source_list, directions, momentum, field, gauge, block_set)

time: 80.4 us -> 79.4 us (0.988)
  local copies, waits for them, and re-layouts: 5.81 us -> 2.63 us
  Pallas kernels: 72.9 us -> 75.2 us
    unnamed x12 -> x2, local copies, waits for them, and re-layouts: 5.81 us -> 2.63 us
    pallas_call x1, Pallas kernels: 72.9 us -> 75.2 us  [per_device(): pl.pallas_call(lambda *refs: kernel(n, nt, *refs), out_shape=(jax.ShapeDt...]
where the time goes in v3:
time: 79.4 us; the launch traced here: 79.1 us
  Pallas kernels  75.2 us (95%)
  local copies, waits for them, and re-layouts  2.63 us (3%)
  between operations  1.29 us (2%)
    pallas_call x1, Pallas kernels, per_device(): pl.pallas_call(lambda *refs: kernel(n, nt, *refs), out_shape=(jax.ShapeDt...  75.2 us
    unnamed x2, local copies, waits for them, and re-layouts  2.63 us

profile of v3, /device:TPU:0, one launch (start us, length us, event | category | flops | bytes accessed | tf_op | source)
XLA Modules:
  0.0 79.1 jit_solution(3682866325498983507)
XLA Ops:
  1.3 75.2 %meson.1 = (bf16[32,2,256]{2,1,0:T(2,128)(2,1)}, f32[2,1,4]{2,1,0:T(1,128)}) custom-call(s32[4]{0:T(128)} %refs_0_.1, s32[1]{0:T(128)S(6)} %copy.10.refs_1_, s32[3]{0:T(128)} %refs_2_.1, bf16[6,8,32,128]{3,2,1,0:T(8,128)(2,1)} %bitcast.5, f32[54,1,128]{2,1,0:T(1,128)} %bitcast.7, bf16[8,2,256,256]{3,2,1,0:T(8,128)(2,1)} %bitcast.4), custom_call_target="tpu_custom_call" | custom-call | tf_op jit(solution)/shard_map/meson/pallas_call | solution.py:593
  76.5 1.4 %copy.11 = bf16[1,32,2,256]{3,2,1,0:T(2,128)(2,1)} copy(bf16[1,32,2,256]{3,2,1,0:T(2,128)(2,1)} %bitcast.6) | data formatting | bytes 65536
  77.9 1.2 %copy.12 = f32[2,1,4]{2,1,0:T(1,128)} copy(f32[2,1,4]{2,1,0:T(1,128)} %get-tuple-element.9) | data formatting | bytes 64

commit v4 on v3

--- a/solution.py
+++ b/solution.py
@@ -127,6 +127,16 @@
     per = n // nt
     layer = me // per
     member = tm_me * per + lax.rem(me, per)
+    half = max(nt // 2, 1)
+
+    def layer_of(timeslice):
+        return lax.rem(timeslice, 2) * half + timeslice // 2
+
+    def slice_of(index):
+        return lax.rem(index, half) * 2 + index // half
+
+    home = layer_of(tm_me)
+    held = slice_of(layer)
     rows = field_ref.shape[2]
     chunk = row_chunk(rows)
     per_plane = rows // chunk
@@ -162,14 +172,14 @@
         pl.semaphore_signal(barrier, inc=1, device_id=device, device_id_type=MESH)
 
     def greet_origin(plane):
-        origin = {"tm": layer, "space": plane}
+        origin = {"tm": held, "space": plane}
 
         @pl.when(jnp.logical_not(is_self(origin)))
         def _():
             greet(origin)
 
     def greet_target(index):
-        target = member_id(tm_me, index)
+        target = member_id(home, index)
 
         @pl.when(jnp.logical_not(is_self(target)))
         def _():
@@ -185,7 +195,7 @@
         gauge_own[k] = gauge_ref[k]
     towards = direction_ref[0].astype(jnp.float32)
     gauge_own[54] = jnp.full((1, lanes), towards, jnp.float32)
-    at_home = jnp.where(layer == tm_me, 1, 0)
+    at_home = jnp.where(held == tm_me, 1, 0)
     pl.semaphore_wait(barrier, 2 * (n - at_home) + n - 1 + n - 1 + nt - 1)
 
     def remote(kind, source, target, device, peer, slot):
@@ -198,22 +208,39 @@
             device_id_type=MESH,
         )
 
-    def gauge_copy(device, peer, slot):
-        return remote(0, gauge_own, gauge_all.at[slot], device, peer, slot)
-
-    def field_copy(device, peer, slot):
-        return remote(1, field_ref.at[:, peer], field_in.at[slot], device, peer, slot)
-
-    def home_copy():
-        return pltpu.make_async_copy(field_ref.at[:, member], field_in.at[me], local_sem)
-
-    def twice_copy(peer, slot):
-        return remote(2, twice.at[peer], twice_in.at[slot], member_id(layer, peer), peer, slot)
-
-    def gradient_copy(peer, slot):
+    def span_of(piece):
+        return pl.ds(pl.multiple_of(piece * chunk, chunk), chunk)
+
+    def gauge_home():
+        return remote(1, gauge_own, gauge_all.at[me], member_id(home, me), 0, 0)
+
+    def gauge_copy(peer, slot):
         return remote(
-            3, gradient.at[peer], gradient_in.at[slot], member_id(layer, peer), peer, slot
+            0, gauge_all.at[slot], gauge_all.at[slot], member_id(layer, peer), peer, slot
         )
+
+    def field_copy(device, peer, slot, piece):
+        span = span_of(piece)
+        source, target = field_ref.at[:, peer, span], field_in.at[slot, :, span]
+        return remote(8 + piece, source, target, device, peer, slot)
+
+    def home_copy(piece):
+        span = span_of(piece)
+        return pltpu.make_async_copy(
+            field_ref.at[:, member, span], field_in.at[me, :, span], local_sem.at[piece]
+        )
+
+    def twice_copy(peer, slot, piece):
+        span = span_of(piece)
+        source, target = twice.at[peer, :, span], twice_in.at[slot, :, span]
+        kind = 8 + per_plane + piece
+        return remote(kind, source, target, member_id(layer, peer), peer, slot)
+
+    def gradient_copy(peer, slot, piece):
+        span = span_of(piece)
+        source, target = gradient.at[peer, :, span], gradient_in.at[slot, :, span]
+        kind = 8 + 2 * per_plane + piece
+        return remote(kind, source, target, member_id(layer, peer), peer, slot)
 
     def part_copy(peer, slot):
         return remote(4, part_send.at[peer], part_in.at[slot], member_id(layer, peer), peer, slot)
@@ -235,27 +262,44 @@
     def arrive_all(copy, mine=member):
         each_peer(lambda peer: copy(peer, peer).wait_recv(), mine=mine)
 
-    def send_gauge(peer):
-        device = member_id(tm_me, peer)
-
-        @pl.when(jnp.logical_not(is_self(device)))
+    gauge_stays = is_self(member_id(home, me))
+
+    @pl.when(jnp.logical_not(gauge_stays))
+    def _():
+        gauge_home().start()
+
+    @pl.when(gauge_stays)
+    def _():
+        gauge_all[me] = gauge_own[...]
+
+    def each_piece(act):
+        def step(piece, carry):
+            act(piece)
+            return carry
+
+        lax.fori_loop(0, per_plane, step, 0)
+
+    def send_fields(piece):
+        def send_field(peer):
+            device = member_id(home, peer)
+
+            @pl.when(jnp.logical_not(is_self(device)))
+            def _():
+                field_copy(device, peer, me, piece).start()
+
+        each_peer(send_field, lead=0)
+
+        @pl.when(held == tm_me)
         def _():
-            gauge_copy(device, peer, me).start()
-
-    def send_field(peer):
-        device = member_id(tm_me, peer)
-
-        @pl.when(jnp.logical_not(is_self(device)))
-        def _():
-            field_copy(device, peer, me).start()
-
-    each_peer(send_gauge, lead=0)
-    each_peer(send_field, lead=0)
-
-    @pl.when(layer == tm_me)
+            home_copy(piece).start()
+
+    each_piece(send_fields)
+
+    @pl.when(jnp.logical_not(is_self({"tm": held, "space": member})))
     def _():
-        home_copy().start()
-        gauge_all[me] = gauge_own[...]
+        gauge_home().wait_recv()
+
+    start_all(gauge_copy)
 
     plane_at = lax.broadcasted_iota(jnp.int32, (n, lanes), 0).astype(jnp.float32)
     site = lax.broadcasted_iota(jnp.int32, (n, lanes), 1)
@@ -271,26 +315,20 @@
     table[0] = jnp.cos(angle)
     table[1] = jnp.sin(angle)
 
-    def take_gauge(plane):
-        origin = {"tm": layer, "space": plane}
-
-        @pl.when(jnp.logical_not(is_self(origin)))
-        def _():
-            gauge_copy(member_id(tm_me, lax.rem(member + 1, n)), plane, plane).wait_recv()
-
-    def take_field(plane):
-        origin = {"tm": layer, "space": plane}
+    def take_field(plane, piece):
+        origin = {"tm": held, "space": plane}
         mine = is_self(origin)
 
         @pl.when(jnp.logical_not(mine))
         def _():
-            field_copy(member_id(tm_me, lax.rem(member + 1, n)), plane, plane).wait_recv()
+            device = member_id(home, lax.rem(member + 1, n))
+            field_copy(device, plane, plane, piece).wait_recv()
 
         @pl.when(mine)
         def _():
-            home_copy().wait()
-
-    each_peer(take_gauge, lead=0)
+            home_copy(piece).wait()
+
+    arrive_all(gauge_copy)
 
     def widen(z, carry):
         for k in range(54):
@@ -385,61 +423,58 @@
             gradient[z, c, span, :] = (cosine * real + sine * imag).astype(jnp.bfloat16)
             gradient[z, 3 + c, span, :] = (cosine * imag - sine * real).astype(jnp.bfloat16)
 
-    def each_piece(act):
-        def step(piece, carry):
-            act(piece)
-            return carry
-
-        lax.fori_loop(0, per_plane, step, 0)
-
     turn = jnp.where(2 * layer < nt, 1, -1)
     begin = jnp.where(2 * layer < nt, layer * per + 1, layer * per)
 
-    def first_plane(d, carry):
-        z = lax.rem(begin + turn * d + n, n)
-
-        @pl.when(d == 0)
-        def _():
-            take_field(lax.rem(z - turn + n, n))
-            take_field(z)
-
-        @pl.when(d < n - 2)
-        def _():
-            take_field(lax.rem(z + turn + n, n))
-
-        each_piece(lambda piece: sweep(field_in, once, z, piece))
-        return carry
-
-    lax.fori_loop(0, n, first_plane, 0)
-
-    def last_plane(d, carry):
-        z = lax.rem(member + d, n)
-        each_piece(lambda piece: sweep(once, twice, z, piece))
-
-        @pl.when(d < n)
-        def _():
-            twice_copy(z, member).start()
-
-        return carry
-
-    lax.fori_loop(1, n + 1, last_plane, 0)
+    def work(piece):
+        def first_plane(d, carry):
+            z = lax.rem(begin + turn * d + n, n)
+
+            @pl.when(d == 0)
+            def _():
+                take_field(lax.rem(z - turn + n, n), piece)
+                take_field(z, piece)
+
+            @pl.when(d < n - 2)
+            def _():
+                take_field(lax.rem(z + turn + n, n), piece)
+
+            sweep(field_in, once, z, piece)
+            return carry
+
+        def last_plane(d, carry):
+            z = lax.rem(member + d, n)
+            sweep(once, twice, z, piece)
+
+            @pl.when(d < n)
+            def _():
+                twice_copy(z, member, piece).start()
+
+            return carry
+
+        def derive_plane(d, carry):
+            z = lax.rem(member + d, n)
+            derive(z, piece)
+
+            @pl.when(d < n)
+            def _():
+                gradient_copy(z, member, piece).start()
+
+            return carry
+
+        lax.fori_loop(0, n, first_plane, 0)
+        lax.fori_loop(1, n + 1, last_plane, 0)
+        lax.fori_loop(1, n + 1, derive_plane, 0)
+
+    each_piece(work)
     twice_in[member] = twice[member]
-
-    def derive_plane(d, carry):
-        z = lax.rem(member + d, n)
-        each_piece(lambda piece: derive(z, piece))
-
-        @pl.when(d < n)
-        def _():
-            gradient_copy(z, member).start()
-
-        return carry
-
-    lax.fori_loop(1, n + 1, derive_plane, 0)
     gradient_in[member] = gradient[member]
 
-    arrive_all(twice_copy)
-    arrive_all(gradient_copy)
+    def arrive_piece(piece):
+        each_peer(lambda peer: twice_copy(peer, peer, piece).wait_recv())
+        each_peer(lambda peer: gradient_copy(peer, peer, piece).wait_recv())
+
+    each_piece(arrive_piece)
     left = jnp.concatenate([flat_rows(twice_in[:, k]) for k in range(6)], axis=1)
     parts = [flat_rows(gradient_in[:, k]) for k in range(6)]
     right_real = jnp.concatenate(parts, axis=1)
@@ -456,7 +491,7 @@
     summed = jnp.sum(part_in[...].astype(jnp.float32), axis=0)
     own = (summed * scale).astype(jnp.bfloat16)
     own_send[...] = own
-    rows_all[layer] = own
+    rows_all[held] = own
 
     def layer_copy(peer, slot):
         return pltpu.make_async_remote_copy(
@@ -469,27 +504,27 @@
         )
 
     def send_sink(plane):
-        device = {"tm": layer, "space": plane}
+        device = {"tm": held, "space": plane}
 
         @pl.when(jnp.logical_not(is_self(device)))
         def _():
             sink_copy(device, plane, member).start()
 
     def take_sink(index):
-        origin = member_id(tm_me, index)
+        origin = member_id(home, index)
 
         @pl.when(jnp.logical_not(is_self(origin)))
         def _():
             sink_copy({"tm": tm_me, "space": lax.rem(me + 1, n)}, index, index).wait_recv()
 
-    each_layer(lambda peer: layer_copy(peer, layer).start())
+    each_layer(lambda peer: layer_copy(peer, held).start())
     each_peer(send_sink, mine=me, lead=0)
 
-    @pl.when(layer == tm_me)
+    @pl.when(held == tm_me)
     def _():
         rows_sink[member] = own_send[...]
 
-    each_layer(lambda peer: layer_copy(peer, peer).wait_recv())
+    each_layer(lambda peer: layer_copy(peer, slice_of(peer)).wait_recv())
     source_send[...] = rows_all[source_ref[layer]]
     start_all(source_copy)
     rows_source[member] = source_send[...]
@@ -553,27 +588,36 @@
     trace_ref[0] = total[0:1, :nt]
     trace_ref[1] = total[1:2, :nt]
 
-    def sent_first(peer):
-        device = member_id(tm_me, peer)
-
-        @pl.when(jnp.logical_not(is_self(device)))
-        def _():
-            gauge_copy(device, peer, me).wait_send()
-            field_copy(device, peer, me).wait_send()
-
-    each_peer(sent_first, lead=0)
+    @pl.when(jnp.logical_not(gauge_stays))
+    def _():
+        gauge_home().wait_send()
+
+    def sent_piece(piece):
+        def sent_field(peer):
+            device = member_id(home, peer)
+
+            @pl.when(jnp.logical_not(is_self(device)))
+            def _():
+                field_copy(device, peer, me, piece).wait_send()
+
+        each_peer(sent_field, lead=0)
+        each_peer(lambda peer: twice_copy(peer, member, piece).wait_send())
+        each_peer(lambda peer: gradient_copy(peer, member, piece).wait_send())
+
+    each_piece(sent_piece)
+
     def sent_sink(plane):
-        device = {"tm": layer, "space": plane}
+        device = {"tm": held, "space": plane}
 
         @pl.when(jnp.logical_not(is_self(device)))
         def _():
             sink_copy(device, plane, member).wait_send()
 
     each_peer(sent_sink, mine=me, lead=0)
-    for copy in (twice_copy, gradient_copy, part_copy, source_copy):
+    for copy in (gauge_copy, part_copy, source_copy):
         each_peer(lambda peer: copy(peer, member).wait_send())
     each_peer(lambda peer: trace_copy(peer, me).wait_send(), mine=me)
-    each_layer(lambda peer: layer_copy(peer, layer).wait_send())
+    each_layer(lambda peer: layer_copy(peer, held).wait_send())
 
 
 def per_device(n, nt, vectors, gauge_links, perambulator, directions, momentum, source_list):
@@ -590,6 +634,7 @@
     anywhere = pl.BlockSpec(memory_space=pltpu.HBM)
     split = (n, 6, rows, lanes)
     count = block_set.shape[0]
+    pieces = rows // row_chunk(rows)
     own, trace = pl.pallas_call(
         lambda *refs: kernel(n, nt, *refs),
         out_shape=(
@@ -621,12 +666,12 @@
             pltpu.VMEM((2 * nv, 2 * nv), bf16),
             pltpu.VMEM((8, 128), f32),
             pltpu.VMEM((n, 8, 128), f32),
-            pltpu.SemaphoreType.DMA((8, n)),
-            pltpu.SemaphoreType.DMA((8, n)),
+            pltpu.SemaphoreType.DMA((8 + 3 * pieces, n)),
+            pltpu.SemaphoreType.DMA((8 + 3 * pieces, n)),
             pltpu.SemaphoreType.DMA((nt,)),
             pltpu.SemaphoreType.DMA((nt,)),
             pltpu.SemaphoreType.DMA,
-            pltpu.SemaphoreType.DMA,
+            pltpu.SemaphoreType.DMA((pieces,)),
         ],
         compiler_params=pltpu.CompilerParams(
             collective_id=0, has_side_effects=True, vmem_limit_bytes=60 * 1024 * 1024

time: 79.4 us -> 67.2 us (0.85)
  Pallas kernels: 75.2 us -> 63 us
    pallas_call x1, Pallas kernels: 75.2 us -> 63 us  [per_device(): pl.pallas_call(lambda *refs: kernel(n, nt, *refs), out_shape=(jax.ShapeDt...]
where the time goes in v4:
time: 67.2 us; the launch traced here: 66.9 us
  Pallas kernels  63 us (94%)
  local copies, waits for them, and re-layouts  2.63 us (4%)
  between operations  1.29 us (2%)
    pallas_call x1, Pallas kernels, per_device(): pl.pallas_call(lambda *refs: kernel(n, nt, *refs), out_shape=(jax.ShapeDt...  63 us
    unnamed x2, local copies, waits for them, and re-layouts  2.63 us

profile of v4, /device:TPU:0, one launch (start us, length us, event | category | flops | bytes accessed | tf_op | source)
XLA Modules:
  0.0 66.9 jit_solution(14926910546906259535)
XLA Ops:
  1.3 63.0 %meson.1 = (bf16[32,2,256]{2,1,0:T(2,128)(2,1)}, f32[2,1,4]{2,1,0:T(1,128)}) custom-call(s32[4]{0:T(128)} %refs_0_.1, s32[1]{0:T(128)S(6)} %copy.10.refs_1_, s32[3]{0:T(128)} %refs_2_.1, bf16[6,8,32,128]{3,2,1,0:T(8,128)(2,1)} %bitcast.5, f32[54,1,128]{2,1,0:T(1,128)} %bitcast.7, bf16[8,2,256,256]{3,2,1,0:T(8,128)(2,1)} %bitcast.4), custom_call_target="tpu_custom_call" | custom-call | tf_op jit(solution)/shard_map/meson/pallas_call | solution.py:638
  64.3 1.4 %copy.11 = bf16[1,32,2,256]{3,2,1,0:T(2,128)(2,1)} copy(bf16[1,32,2,256]{3,2,1,0:T(2,128)(2,1)} %bitcast.6) | data formatting | bytes 65536
  65.7 1.2 %copy.12 = f32[2,1,4]{2,1,0:T(1,128)} copy(f32[2,1,4]{2,1,0:T(1,128)} %get-tuple-element.9) | data formatting | bytes 64

commit v5 on v4

--- a/solution.py
+++ b/solution.py
@@ -195,112 +195,6 @@
         gauge_own[k] = gauge_ref[k]
     towards = direction_ref[0].astype(jnp.float32)
     gauge_own[54] = jnp.full((1, lanes), towards, jnp.float32)
-    at_home = jnp.where(held == tm_me, 1, 0)
-    pl.semaphore_wait(barrier, 2 * (n - at_home) + n - 1 + n - 1 + nt - 1)
-
-    def remote(kind, source, target, device, peer, slot):
-        return pltpu.make_async_remote_copy(
-            src_ref=source,
-            dst_ref=target,
-            send_sem=send_sem.at[kind, peer],
-            recv_sem=recv_sem.at[kind, slot],
-            device_id=device,
-            device_id_type=MESH,
-        )
-
-    def span_of(piece):
-        return pl.ds(pl.multiple_of(piece * chunk, chunk), chunk)
-
-    def gauge_home():
-        return remote(1, gauge_own, gauge_all.at[me], member_id(home, me), 0, 0)
-
-    def gauge_copy(peer, slot):
-        return remote(
-            0, gauge_all.at[slot], gauge_all.at[slot], member_id(layer, peer), peer, slot
-        )
-
-    def field_copy(device, peer, slot, piece):
-        span = span_of(piece)
-        source, target = field_ref.at[:, peer, span], field_in.at[slot, :, span]
-        return remote(8 + piece, source, target, device, peer, slot)
-
-    def home_copy(piece):
-        span = span_of(piece)
-        return pltpu.make_async_copy(
-            field_ref.at[:, member, span], field_in.at[me, :, span], local_sem.at[piece]
-        )
-
-    def twice_copy(peer, slot, piece):
-        span = span_of(piece)
-        source, target = twice.at[peer, :, span], twice_in.at[slot, :, span]
-        kind = 8 + per_plane + piece
-        return remote(kind, source, target, member_id(layer, peer), peer, slot)
-
-    def gradient_copy(peer, slot, piece):
-        span = span_of(piece)
-        source, target = gradient.at[peer, :, span], gradient_in.at[slot, :, span]
-        kind = 8 + 2 * per_plane + piece
-        return remote(kind, source, target, member_id(layer, peer), peer, slot)
-
-    def part_copy(peer, slot):
-        return remote(4, part_send.at[peer], part_in.at[slot], member_id(layer, peer), peer, slot)
-
-    def sink_copy(device, peer, slot):
-        return remote(5, own_send, rows_sink.at[slot], device, peer, slot)
-
-    def source_copy(peer, slot):
-        return remote(6, source_send, rows_source.at[slot], member_id(layer, peer), peer, slot)
-
-    def trace_copy(peer, slot):
-        return remote(
-            7, trace_send, trace_in.at[slot], {"tm": tm_me, "space": peer}, peer, slot
-        )
-
-    def start_all(copy, mine=member):
-        each_peer(lambda peer: copy(peer, mine).start(), mine=mine)
-
-    def arrive_all(copy, mine=member):
-        each_peer(lambda peer: copy(peer, peer).wait_recv(), mine=mine)
-
-    gauge_stays = is_self(member_id(home, me))
-
-    @pl.when(jnp.logical_not(gauge_stays))
-    def _():
-        gauge_home().start()
-
-    @pl.when(gauge_stays)
-    def _():
-        gauge_all[me] = gauge_own[...]
-
-    def each_piece(act):
-        def step(piece, carry):
-            act(piece)
-            return carry
-
-        lax.fori_loop(0, per_plane, step, 0)
-
-    def send_fields(piece):
-        def send_field(peer):
-            device = member_id(home, peer)
-
-            @pl.when(jnp.logical_not(is_self(device)))
-            def _():
-                field_copy(device, peer, me, piece).start()
-
-        each_peer(send_field, lead=0)
-
-        @pl.when(held == tm_me)
-        def _():
-            home_copy(piece).start()
-
-    each_piece(send_fields)
-
-    @pl.when(jnp.logical_not(is_self({"tm": held, "space": member})))
-    def _():
-        gauge_home().wait_recv()
-
-    start_all(gauge_copy)
-
     plane_at = lax.broadcasted_iota(jnp.int32, (n, lanes), 0).astype(jnp.float32)
     site = lax.broadcasted_iota(jnp.int32, (n, lanes), 1)
     angle = (
@@ -314,6 +208,112 @@
     )
     table[0] = jnp.cos(angle)
     table[1] = jnp.sin(angle)
+    at_home = jnp.where(held == tm_me, 1, 0)
+    pl.semaphore_wait(barrier, 2 * (n - at_home) + n - 1 + n - 1 + nt - 1)
+
+    def remote(kind, source, target, device, peer, slot):
+        return pltpu.make_async_remote_copy(
+            src_ref=source,
+            dst_ref=target,
+            send_sem=send_sem.at[kind, peer],
+            recv_sem=recv_sem.at[kind, slot],
+            device_id=device,
+            device_id_type=MESH,
+        )
+
+    def span_of(piece):
+        return pl.ds(pl.multiple_of(piece * chunk, chunk), chunk)
+
+    def gauge_home():
+        return remote(1, gauge_own, gauge_all.at[me], member_id(home, me), 0, 0)
+
+    def gauge_copy(peer, slot):
+        return remote(
+            0, gauge_all.at[slot], gauge_all.at[slot], member_id(layer, peer), peer, slot
+        )
+
+    def field_copy(device, peer, slot, piece):
+        span = span_of(piece)
+        source, target = field_ref.at[:, peer, span], field_in.at[slot, :, span]
+        return remote(8 + piece, source, target, device, peer, slot)
+
+    def home_copy(piece):
+        span = span_of(piece)
+        return pltpu.make_async_copy(
+            field_ref.at[:, member, span], field_in.at[me, :, span], local_sem.at[piece]
+        )
+
+    def twice_copy(peer, slot, piece):
+        span = span_of(piece)
+        source, target = twice.at[peer, :, span], twice_in.at[slot, :, span]
+        kind = 8 + per_plane + piece
+        return remote(kind, source, target, member_id(layer, peer), peer, slot)
+
+    def gradient_copy(peer, slot, piece):
+        span = span_of(piece)
+        source, target = gradient.at[peer, :, span], gradient_in.at[slot, :, span]
+        kind = 8 + 2 * per_plane + piece
+        return remote(kind, source, target, member_id(layer, peer), peer, slot)
+
+    def part_copy(peer, slot):
+        return remote(4, part_send.at[peer], part_in.at[slot], member_id(layer, peer), peer, slot)
+
+    def sink_copy(device, peer, slot):
+        return remote(5, own_send, rows_sink.at[slot], device, peer, slot)
+
+    def source_copy(peer, slot):
+        return remote(6, source_send, rows_source.at[slot], member_id(layer, peer), peer, slot)
+
+    def trace_copy(peer, slot):
+        return remote(
+            7, trace_send, trace_in.at[slot], {"tm": tm_me, "space": peer}, peer, slot
+        )
+
+    def start_all(copy, mine=member):
+        each_peer(lambda peer: copy(peer, mine).start(), mine=mine)
+
+    def arrive_all(copy, mine=member):
+        each_peer(lambda peer: copy(peer, peer).wait_recv(), mine=mine)
+
+    gauge_stays = is_self(member_id(home, me))
+
+    @pl.when(jnp.logical_not(gauge_stays))
+    def _():
+        gauge_home().start()
+
+    @pl.when(gauge_stays)
+    def _():
+        gauge_all[me] = gauge_own[...]
+
+    def each_piece(act):
+        def step(piece, carry):
+            act(piece)
+            return carry
+
+        lax.fori_loop(0, per_plane, step, 0)
+
+    def send_fields(piece):
+        def send_field(peer):
+            device = member_id(home, peer)
+
+            @pl.when(jnp.logical_not(is_self(device)))
+            def _():
+                field_copy(device, peer, me, piece).start()
+
+        each_peer(send_field, lead=0)
+
+        @pl.when(held == tm_me)
+        def _():
+            home_copy(piece).start()
+
+    each_piece(send_fields)
+
+    @pl.when(jnp.logical_not(is_self({"tm": held, "space": member})))
+    def _():
+        gauge_home().wait_recv()
+
+    start_all(gauge_copy)
+
 
     def take_field(plane, piece):
         origin = {"tm": held, "space": plane}
@@ -426,45 +426,54 @@
     turn = jnp.where(2 * layer < nt, 1, -1)
     begin = jnp.where(2 * layer < nt, layer * per + 1, layer * per)
 
+    step = 2 if n % 2 == 0 else 1
+
     def work(piece):
-        def first_plane(d, carry):
-            z = lax.rem(begin + turn * d + n, n)
-
-            @pl.when(d == 0)
+        def first_planes(e, carry):
+            group = [lax.rem(begin + turn * (e * step + g) + n, n) for g in range(step)]
+
+            @pl.when(e == 0)
             def _():
-                take_field(lax.rem(z - turn + n, n), piece)
-                take_field(z, piece)
-
-            @pl.when(d < n - 2)
-            def _():
-                take_field(lax.rem(z + turn + n, n), piece)
-
-            sweep(field_in, once, z, piece)
+                take_field(lax.rem(group[0] - turn + n, n), piece)
+                take_field(group[0], piece)
+
+            for g, z in enumerate(group):
+
+                @pl.when(e * step + g < n - 2)
+                def _(z=z):
+                    take_field(lax.rem(z + turn + n, n), piece)
+
+            for z in group:
+                sweep(field_in, once, z, piece)
             return carry
 
-        def last_plane(d, carry):
-            z = lax.rem(member + d, n)
-            sweep(once, twice, z, piece)
-
-            @pl.when(d < n)
-            def _():
-                twice_copy(z, member, piece).start()
+        def last_planes(e, carry):
+            group = [lax.rem(member + e * step + g + 1, n) for g in range(step)]
+            for z in group:
+                sweep(once, twice, z, piece)
+            for g, z in enumerate(group):
+
+                @pl.when(e * step + g + 1 < n)
+                def _(z=z):
+                    twice_copy(z, member, piece).start()
 
             return carry
 
-        def derive_plane(d, carry):
-            z = lax.rem(member + d, n)
-            derive(z, piece)
-
-            @pl.when(d < n)
-            def _():
-                gradient_copy(z, member, piece).start()
+        def derive_planes(e, carry):
+            group = [lax.rem(member + e * step + g + 1, n) for g in range(step)]
+            for z in group:
+                derive(z, piece)
+            for g, z in enumerate(group):
+
+                @pl.when(e * step + g + 1 < n)
+                def _(z=z):
+                    gradient_copy(z, member, piece).start()
 
             return carry
 
-        lax.fori_loop(0, n, first_plane, 0)
-        lax.fori_loop(1, n + 1, last_plane, 0)
-        lax.fori_loop(1, n + 1, derive_plane, 0)
+        lax.fori_loop(0, n // step, first_planes, 0)
+        lax.fori_loop(0, n // step, last_planes, 0)
+        lax.fori_loop(0, n // step, derive_planes, 0)
 
     each_piece(work)
     twice_in[member] = twice[member]
@@ -536,7 +545,9 @@
     own_ref[:, 1, :] = mine_rows[:, nv:].astype(jnp.bfloat16)
     sink = flat_rows(rows_sink[...])
 
-    def first_block(q, carry):
+    pair = 2 if blocks.shape[0] % 2 == 0 else 1
+
+    def first_block(q):
         real = blocks[q, 0]
         imag = blocks[q, 1]
         tall = jnp.concatenate([real, -imag], axis=0)
@@ -547,9 +558,13 @@
         firsts[q, :, nv:] = jnp.dot(sink, tall_imag, preferred_element_type=jnp.float32).astype(
             jnp.bfloat16
         )
+
+    def first_blocks(e, carry):
+        for g in range(pair):
+            first_block(e * pair + g)
         return carry
 
-    lax.fori_loop(0, blocks.shape[0], first_block, 0)
+    lax.fori_loop(0, blocks.shape[0] // pair, first_blocks, 0)
     arrive_all(source_copy)
     partner = flat_rows(rows_source[...])
     partner_real, partner_imag = partner[:, :nv], partner[:, nv:]
@@ -561,8 +576,7 @@
     def fold(values):
         return jnp.sum(values.reshape(nv // 8, 8, nv), axis=0)
 
-    def second_block(q, carry):
-        sum_real, sum_imag = carry
+    def second_block(q, sum_real, sum_imag):
         second = jnp.dot(firsts[q], right_side[...], preferred_element_type=jnp.float32)
         second_real, second_imag = second[:, :nv], second[:, nv:]
         real = blocks[q, 0].astype(jnp.float32)
@@ -571,8 +585,15 @@
         sum_imag = sum_imag + fold(second_imag * real - second_real * imag)
         return sum_real, sum_imag
 
+    def second_blocks(e, carry):
+        for g in range(pair):
+            carry = second_block(e * pair + g, *carry)
+        return carry
+
     nothing = jnp.zeros((8, nv), jnp.float32)
-    sum_real, sum_imag = lax.fori_loop(0, blocks.shape[0], second_block, (nothing, nothing))
+    sum_real, sum_imag = lax.fori_loop(
+        0, blocks.shape[0] // pair, second_blocks, (nothing, nothing)
+    )
     trace_real = jnp.sum(sum_real)
     trace_imag = jnp.sum(sum_imag)
     row = lax.broadcasted_iota(jnp.int32, trace_send.shape, 0)

time: 67.2 us -> 65.8 us (0.979)
  Pallas kernels: 63 us -> 61.6 us
    pallas_call x1, Pallas kernels: 63 us -> 61.6 us  [per_device(): pl.pallas_call(lambda *refs: kernel(n, nt, *refs), out_shape=(jax.ShapeDt...]
where the time goes in v5:
time: 65.8 us; the launch traced here: 65.5 us
  Pallas kernels  61.6 us (94%)
  local copies, waits for them, and re-layouts  2.63 us (4%)
  between operations  1.29 us (2%)
    pallas_call x1, Pallas kernels, per_device(): pl.pallas_call(lambda *refs: kernel(n, nt, *refs), out_shape=(jax.ShapeDt...  61.6 us
    unnamed x2, local copies, waits for them, and re-layouts  2.63 us

profile of v5, /device:TPU:0, one launch (start us, length us, event | category | flops | bytes accessed | tf_op | source)
XLA Modules:
  0.0 65.5 jit_solution(10572607388641530226)
XLA Ops:
  1.3 61.6 %meson.1 = (bf16[32,2,256]{2,1,0:T(2,128)(2,1)}, f32[2,1,4]{2,1,0:T(1,128)}) custom-call(s32[4]{0:T(128)} %refs_0_.1, s32[1]{0:T(128)S(6)} %copy.10.refs_1_, s32[3]{0:T(128)} %refs_2_.1, bf16[6,8,32,128]{3,2,1,0:T(8,128)(2,1)} %bitcast.5, f32[54,1,128]{2,1,0:T(1,128)} %bitcast.7, bf16[8,2,256,256]{3,2,1,0:T(8,128)(2,1)} %bitcast.4), custom_call_target="tpu_custom_call" | custom-call | tf_op jit(solution)/shard_map/meson/pallas_call | solution.py:659
  62.9 1.4 %copy.11 = bf16[1,32,2,256]{3,2,1,0:T(2,128)(2,1)} copy(bf16[1,32,2,256]{3,2,1,0:T(2,128)(2,1)} %bitcast.6) | data formatting | bytes 65536
  64.3 1.2 %copy.12 = f32[2,1,4]{2,1,0:T(1,128)} copy(f32[2,1,4]{2,1,0:T(1,128)} %get-tuple-element.9) | data formatting | bytes 64

commit v6 on v5

--- a/solution.py
+++ b/solution.py
@@ -137,9 +137,9 @@
 
     home = layer_of(tm_me)
     held = slice_of(layer)
-    rows = field_ref.shape[2]
-    chunk = row_chunk(rows)
-    per_plane = rows // chunk
+    per_plane, chunk = field_ref.shape[1], field_ref.shape[3]
+    rows = per_plane * chunk
+    width = n * chunk
     lanes = SX * SY
     nv = n * rows
 
@@ -234,13 +234,13 @@
 
     def field_copy(device, peer, slot, piece):
         span = span_of(piece)
-        source, target = field_ref.at[:, peer, span], field_in.at[slot, :, span]
+        source, target = field_ref.at[:, piece, peer], field_in.at[slot, :, span]
         return remote(8 + piece, source, target, device, peer, slot)
 
     def home_copy(piece):
         span = span_of(piece)
         return pltpu.make_async_copy(
-            field_ref.at[:, member, span], field_in.at[me, :, span], local_sem.at[piece]
+            field_ref.at[:, piece, member], field_in.at[me, :, span], local_sem.at[piece]
         )
 
     def twice_copy(peer, slot, piece):
@@ -255,11 +255,16 @@
         kind = 8 + 2 * per_plane + piece
         return remote(kind, source, target, member_id(layer, peer), peer, slot)
 
-    def part_copy(peer, slot):
-        return remote(4, part_send.at[peer], part_in.at[slot], member_id(layer, peer), peer, slot)
-
-    def sink_copy(device, peer, slot):
-        return remote(5, own_send, rows_sink.at[slot], device, peer, slot)
+    def part_copy(peer, slot, piece):
+        source, target = part_send.at[piece, peer], part_in.at[piece, slot]
+        kind = 8 + 3 * per_plane + piece
+        return remote(kind, source, target, member_id(layer, peer), peer, slot)
+
+    def sink_copy(device, peer, slot, piece):
+        kind = 8 + 4 * per_plane + piece
+        return remote(
+            kind, own_send.at[piece], rows_sink.at[piece, slot], device, peer, slot
+        )
 
     def source_copy(peer, slot):
         return remote(6, source_send, rows_source.at[slot], member_id(layer, peer), peer, slot)
@@ -479,71 +484,94 @@
     twice_in[member] = twice[member]
     gradient_in[member] = gradient[member]
 
-    def arrive_piece(piece):
+    def piece_rows(held_ref, k, piece):
+        return flat_rows(held_ref[:, k, piece * chunk : (piece + 1) * chunk, :])
+
+    for piece in range(per_plane):
         each_peer(lambda peer: twice_copy(peer, peer, piece).wait_recv())
+    left = jnp.concatenate(
+        [
+            jnp.concatenate([piece_rows(twice_in, k, piece) for k in range(6)], axis=1)
+            for piece in range(per_plane)
+        ],
+        axis=0,
+    )
+    nt_dims = (((1,), (1,)), ((), ()))
+    for piece in range(per_plane):
         each_peer(lambda peer: gradient_copy(peer, peer, piece).wait_recv())
-
-    each_piece(arrive_piece)
-    left = jnp.concatenate([flat_rows(twice_in[:, k]) for k in range(6)], axis=1)
-    parts = [flat_rows(gradient_in[:, k]) for k in range(6)]
-    right_real = jnp.concatenate(parts, axis=1)
-    right_imag = jnp.concatenate(parts[3:] + [-part for part in parts[:3]], axis=1)
-    nt_dims = (((1,), (1,)), ((), ()))
-    sum_real = lax.dot_general(left, right_real, nt_dims, preferred_element_type=jnp.float32)
-    sum_imag = lax.dot_general(left, right_imag, nt_dims, preferred_element_type=jnp.float32)
-    part_send[:, :, :nv] = sum_real.reshape(n, rows, nv).astype(jnp.bfloat16)
-    part_send[:, :, nv:] = sum_imag.reshape(n, rows, nv).astype(jnp.bfloat16)
-    part_in[member] = part_send[member]
-    start_all(part_copy)
-    arrive_all(part_copy)
-    scale = 1.0 / math.sqrt(3 * SX * SY * n)
-    summed = jnp.sum(part_in[...].astype(jnp.float32), axis=0)
-    own = (summed * scale).astype(jnp.bfloat16)
-    own_send[...] = own
-    rows_all[held] = own
-
-    def layer_copy(peer, slot):
+        parts = [piece_rows(gradient_in, k, piece) for k in range(6)]
+        right_real = jnp.concatenate(parts, axis=1)
+        right_imag = jnp.concatenate(parts[3:] + [-part for part in parts[:3]], axis=1)
+        right = jnp.concatenate([right_real, right_imag], axis=0)
+        part = lax.dot_general(left, right, nt_dims, preferred_element_type=jnp.float32)
+        part_send[piece] = part.reshape(n, rows, 2 * width).astype(jnp.bfloat16)
+        part_in[piece, member] = part_send[piece, member]
+        each_peer(lambda peer: part_copy(peer, member, piece).start())
+
+    def layer_copy(peer, slot, piece):
         return pltpu.make_async_remote_copy(
-            src_ref=own_send,
-            dst_ref=rows_all.at[slot],
-            send_sem=tm_send_sem.at[peer],
-            recv_sem=tm_recv_sem.at[slot],
+            src_ref=own_send.at[piece],
+            dst_ref=rows_all.at[piece, slot],
+            send_sem=tm_send_sem.at[piece, peer],
+            recv_sem=tm_recv_sem.at[piece, slot],
             device_id=member_id(peer, member),
             device_id_type=MESH,
         )
 
-    def send_sink(plane):
-        device = {"tm": held, "space": plane}
-
-        @pl.when(jnp.logical_not(is_self(device)))
+    scale = 1.0 / math.sqrt(3 * SX * SY * n)
+    for piece in range(per_plane):
+        each_peer(lambda peer: part_copy(peer, peer, piece).wait_recv())
+        summed = jnp.sum(part_in[piece].astype(jnp.float32), axis=0)
+        own = (summed * scale).astype(jnp.bfloat16)
+        own_send[piece] = own
+        rows_all[piece, held] = own
+
+        def send_sink(plane):
+            device = {"tm": held, "space": plane}
+
+            @pl.when(jnp.logical_not(is_self(device)))
+            def _():
+                sink_copy(device, plane, member, piece).start()
+
+        each_layer(lambda peer: layer_copy(peer, held, piece).start())
+        each_peer(send_sink, mine=me, lead=0)
+
+        @pl.when(held == tm_me)
         def _():
-            sink_copy(device, plane, member).start()
-
-    def take_sink(index):
+            rows_sink[piece, member] = own_send[piece]
+
+    def take_sink(index, piece):
         origin = member_id(home, index)
 
         @pl.when(jnp.logical_not(is_self(origin)))
         def _():
-            sink_copy({"tm": tm_me, "space": lax.rem(me + 1, n)}, index, index).wait_recv()
-
-    each_layer(lambda peer: layer_copy(peer, held).start())
-    each_peer(send_sink, mine=me, lead=0)
-
-    @pl.when(held == tm_me)
-    def _():
-        rows_sink[member] = own_send[...]
-
-    each_layer(lambda peer: layer_copy(peer, slice_of(peer)).wait_recv())
-    source_send[...] = rows_all[source_ref[layer]]
+            device = {"tm": tm_me, "space": lax.rem(me + 1, n)}
+            sink_copy(device, index, index, piece).wait_recv()
+
+    for piece in range(per_plane):
+        each_layer(lambda peer: layer_copy(peer, slice_of(peer), piece).wait_recv())
+    for piece in range(per_plane):
+        source_send[piece] = rows_all[piece, source_ref[layer]]
     start_all(source_copy)
     rows_source[member] = source_send[...]
-    each_peer(take_sink, lead=0)
+
+    def whole_rows(halves):
+        real = [part[:, :width] for part in halves]
+        imag = [part[:, width:] for part in halves]
+        return jnp.concatenate(real, axis=1), jnp.concatenate(imag, axis=1)
+
+    for piece in range(per_plane):
+        each_peer(lambda index: take_sink(index, piece), lead=0)
     load_blocks.wait()
 
-    mine_rows = rows_sink[me].astype(jnp.float32)
-    own_ref[:, 0, :] = mine_rows[:, :nv].astype(jnp.bfloat16)
-    own_ref[:, 1, :] = mine_rows[:, nv:].astype(jnp.bfloat16)
-    sink = flat_rows(rows_sink[...])
+    mine_real, mine_imag = whole_rows(
+        [rows_sink[piece, me].astype(jnp.float32) for piece in range(per_plane)]
+    )
+    own_ref[:, 0, :] = mine_real.astype(jnp.bfloat16)
+    own_ref[:, 1, :] = mine_imag.astype(jnp.bfloat16)
+    sink = jnp.concatenate(
+        whole_rows([flat_rows(rows_sink[piece]) for piece in range(per_plane)]), axis=1
+    )
 
     pair = 2 if blocks.shape[0] % 2 == 0 else 1
 
@@ -566,8 +594,9 @@
 
     lax.fori_loop(0, blocks.shape[0] // pair, first_blocks, 0)
     arrive_all(source_copy)
-    partner = flat_rows(rows_source[...])
-    partner_real, partner_imag = partner[:, :nv], partner[:, nv:]
+    partner_real, partner_imag = whole_rows(
+        [flat_rows(rows_source[:, piece]) for piece in range(per_plane)]
+    )
     right_side[:nv, :nv] = partner_real
     right_side[:nv, nv:] = partner_imag
     right_side[nv:, :nv] = -partner_imag
@@ -632,20 +661,26 @@
 
         @pl.when(jnp.logical_not(is_self(device)))
         def _():
-            sink_copy(device, plane, member).wait_send()
+            for piece in range(per_plane):
+                sink_copy(device, plane, member, piece).wait_send()
 
     each_peer(sent_sink, mine=me, lead=0)
-    for copy in (gauge_copy, part_copy, source_copy):
+    for copy in (gauge_copy, source_copy):
         each_peer(lambda peer: copy(peer, member).wait_send())
     each_peer(lambda peer: trace_copy(peer, me).wait_send(), mine=me)
-    each_layer(lambda peer: layer_copy(peer, held).wait_send())
+    for piece in range(per_plane):
+        each_peer(lambda peer: part_copy(peer, member, piece).wait_send())
+        each_layer(lambda peer: layer_copy(peer, held, piece).wait_send())
 
 
 def per_device(n, nt, vectors, gauge_links, perambulator, directions, momentum, source_list):
     nv = vectors.shape[4]
     lanes = vectors.shape[5]
     rows = nv // n
-    field = vectors.reshape(6, n, rows, lanes)
+    chunk = row_chunk(rows)
+    pieces = rows // chunk
+    width = n * chunk
+    field = vectors.reshape(6, pieces, n, chunk, lanes)
     gauge = gauge_links.reshape(54, 1, lanes)
     block_set = perambulator[0]
 
@@ -655,7 +690,6 @@
     anywhere = pl.BlockSpec(memory_space=pltpu.HBM)
     split = (n, 6, rows, lanes)
     count = block_set.shape[0]
-    pieces = rows // row_chunk(rows)
     own, trace = pl.pallas_call(
         lambda *refs: kernel(n, nt, *refs),
         out_shape=(
@@ -675,22 +709,22 @@
             pltpu.VMEM(split, bf16),
             pltpu.VMEM(split, bf16),
             pltpu.VMEM(split, bf16),
-            pltpu.VMEM((n, rows, 2 * nv), bf16),
-            pltpu.VMEM((n, rows, 2 * nv), bf16),
-            pltpu.VMEM((rows, 2 * nv), bf16),
-            pltpu.VMEM((nt, rows, 2 * nv), bf16),
-            pltpu.VMEM((n, rows, 2 * nv), bf16),
-            pltpu.VMEM((rows, 2 * nv), bf16),
-            pltpu.VMEM((n, rows, 2 * nv), bf16),
+            pltpu.VMEM((pieces, n, rows, 2 * width), bf16),
+            pltpu.VMEM((pieces, n, rows, 2 * width), bf16),
+            pltpu.VMEM((pieces, rows, 2 * width), bf16),
+            pltpu.VMEM((pieces, nt, rows, 2 * width), bf16),
+            pltpu.VMEM((pieces, n, rows, 2 * width), bf16),
+            pltpu.VMEM((pieces, rows, 2 * width), bf16),
+            pltpu.VMEM((n, pieces, rows, 2 * width), bf16),
             pltpu.VMEM((count, 2, nv, nv), bf16),
             pltpu.VMEM((count, nv, 2 * nv), bf16),
             pltpu.VMEM((2 * nv, 2 * nv), bf16),
             pltpu.VMEM((8, 128), f32),
             pltpu.VMEM((n, 8, 128), f32),
-            pltpu.SemaphoreType.DMA((8 + 3 * pieces, n)),
-            pltpu.SemaphoreType.DMA((8 + 3 * pieces, n)),
-            pltpu.SemaphoreType.DMA((nt,)),
-            pltpu.SemaphoreType.DMA((nt,)),
+            pltpu.SemaphoreType.DMA((8 + 5 * pieces, n)),
+            pltpu.SemaphoreType.DMA((8 + 5 * pieces, n)),
+            pltpu.SemaphoreType.DMA((pieces, nt)),
+            pltpu.SemaphoreType.DMA((pieces, nt)),
             pltpu.SemaphoreType.DMA,
             pltpu.SemaphoreType.DMA((pieces,)),
         ],

time: 65.8 us -> 64.7 us (0.983)
  Pallas kernels: 61.6 us -> 60.6 us
    pallas_call x1, Pallas kernels: 61.6 us -> 60.6 us  [per_device(): pl.pallas_call(lambda *refs: kernel(n, nt, *refs), out_shape=(jax.ShapeDt...]
where the time goes in v6:
time: 64.7 us; the launch traced here: 64.5 us
  Pallas kernels  60.6 us (94%)
  local copies, waits for them, and re-layouts  2.63 us (4%)
  between operations  1.29 us (2%)
    pallas_call x1, Pallas kernels, per_device(): pl.pallas_call(lambda *refs: kernel(n, nt, *refs), out_shape=(jax.ShapeDt...  60.6 us
    unnamed x2, local copies, waits for them, and re-layouts  2.63 us

profile of v6, /device:TPU:0, one launch (start us, length us, event | category | flops | bytes accessed | tf_op | source)
XLA Modules:
  0.0 64.5 jit_solution(10857016851815949293)
XLA Ops:
  1.3 60.6 %meson.1 = (bf16[32,2,256]{2,1,0:T(2,128)(2,1)}, f32[2,1,4]{2,1,0:T(1,128)}) custom-call(s32[4]{0:T(128)} %refs_0_.1, s32[1]{0:T(128)S(6)} %copy.10.refs_1_, s32[3]{0:T(128)} %refs_2_.1, bf16[6,2,8,16,128]{4,3,2,1,0:T(8,128)(2,1)} %bitcast.5, f32[54,1,128]{2,1,0:T(1,128)} %bitcast.7, bf16[8,2,256,256]{3,2,1,0:T(8,128)(2,1)} %bitcast.4), custom_call_target="tpu_custom_call" | custom-call | tf_op jit(solution)/shard_map/meson/pallas_call | solution.py:693
  61.9 1.4 %copy.11 = bf16[1,32,2,256]{3,2,1,0:T(2,128)(2,1)} copy(bf16[1,32,2,256]{3,2,1,0:T(2,128)(2,1)} %bitcast.6) | data formatting | bytes 65536
  63.2 1.2 %copy.12 = f32[2,1,4]{2,1,0:T(1,128)} copy(f32[2,1,4]{2,1,0:T(1,128)} %get-tuple-element.9) | data formatting | bytes 64
